TPU v7x, 32 devices: a whole 2x2x4 slice. The times are simulated.
32 devices in a mesh: seq: 8 (over y, x, core), head: 4 (over z).
Axes of the slice: x: 2, y: 2, z: 4, core: 2. Of those that a mesh axis runs over, the one named last changes fastest.
Arguments:
- query_state: bfloat16 [12288, 512], P('seq'), may hold values from -6 to 6
- content: bfloat16 [12288, 512], P('seq'), may hold values from -6 to 6
- encoded: bfloat16 [12288, 512], P('seq'), may hold values from -6 to 6
- sentence_lengths: int32 [217], replicated, may hold values from 4 to 1024, as said below
- key_score: int32 [12288], replicated, may hold values from 0 to 63
- query_cut: int32 [12288], replicated, may hold values from 1 to 64
- w_query: bfloat16 [512, 512], P(None, 'head'), may hold values from -0.625 to 0.625
- w_key: bfloat16 [512, 512], P(None, 'head'), may hold values from -0.25 to 0.25
- w_value: bfloat16 [512, 512], P(None, 'head'), may hold values from -0.25 to 0.25
- w_out: bfloat16 [512, 512], P('head'), may hold values from -1.5 to 1.5
- gain_self: float32 [512], replicated, may hold values from 0.5 to 1.5
- w_cross_query: bfloat16 [512, 512], P(None, 'head'), may hold values from -0.625 to 0.625
- w_cross_key: bfloat16 [512, 512], P(None, 'head'), may hold values from -0.25 to 0.25
- w_cross_value: bfloat16 [512, 512], P(None, 'head'), may hold values from -0.25 to 0.25
- w_cross_out: bfloat16 [512, 512], P('head'), may hold values from -1.5 to 1.5
- gain_cross: float32 [512], replicated, may hold values from 0.5 to 1.5
- w_inner: bfloat16 [512, 2048], P(None, 'head'), may hold values from -0.25 to 0.25
- w_outer: bfloat16 [2048, 512], P('head'), may hold values from -0.1875 to 0.1875
- gain_final: float32 [512], replicated, may hold values from 0.5 to 1.5
- out_grad: bfloat16 [12288, 512], P('seq'), may hold values from -6 to 6
Outputs:
- mixed: bfloat16 [12288, 512], P('seq')
- query_state_grad: float32 [12288, 512], P('seq')
- content_grad: float32 [12288, 512], P('seq')
- encoded_grad: float32 [12288, 512], P('seq')
- w_query_grad: float32 [512, 512], P(None, 'head')
- w_key_grad: float32 [512, 512], P(None, 'head')
- w_value_grad: float32 [512, 512], P(None, 'head')
- w_out_grad: float32 [512, 512], P('head')
- gain_self_grad: float32 [512], replicated
- w_cross_query_grad: float32 [512, 512], P(None, 'head')
- w_cross_key_grad: float32 [512, 512], P(None, 'head')
- w_cross_value_grad: float32 [512, 512], P(None, 'head')
- w_cross_out_grad: float32 [512, 512], P('head')
- gain_cross_grad: float32 [512], replicated
- w_inner_grad: float32 [512, 2048], P(None, 'head')
- w_outer_grad: float32 [2048, 512], P('head')
- gain_final_grad: float32 [512], replicated
Inputs may be any that keep to these rules, and one draw needn't show every extreme that they name: `sentence_lengths`: exactly 6 entries equal 1024 (the documents); every other entry is a sentence of 4 to 56 tokens, one of them exactly 4; the entries sum to 12288; the order is drawn from the seed.
All inputs are finite; a program needn't handle non-finite values.
Results may differ from a plain program's by a relative error of at most 0.029.
The roundings to bfloat16 on the way count: a program that leaves them out, or rounds other values in their place, can miss the bound.
Values may be sent and summed in bfloat16 or wider, within the bound.
A program may use at most 384 MiB of HBM per device.

v0:
```python
from functools import partial
import math

import jax
import jax.numpy as jnp
from jax import lax
from jax.sharding import PartitionSpec as P

HEAD_SIZE = 64
DOC_LEN = 1024
LEVELS = 64


eps_norm = 1e-05
neg_big = -1e30


def from_behind(value, axis, by):
    peers = lax.axis_size(axis)
    pairs = [(i, i + by) for i in range(peers) if 0 <= i + by < peers]
    return lax.ppermute(value, axis, pairs)


def forward_product(left, right):
    return jnp.dot(left, right, preferred_element_type=jnp.float32)


def rows_product(left, right):
    return jnp.einsum("ti,tj->ij", left, right, preferred_element_type=jnp.float32)


def weight_back(grad, weight):
    return jnp.einsum("tj,ij->ti", grad, weight, preferred_element_type=jnp.float32)


def sentence_of(positions, lengths):
    ends = jnp.cumsum(lengths)
    passed = (positions[:, None] >= ends[None, :]).astype(jnp.int32)
    sentence = jnp.sum(passed, axis=1)
    first = jnp.sum(passed * lengths[None, :], axis=1)
    return (sentence, first)


def layer_norm(resid, gain):
    mean_row = jnp.mean(resid, axis=1, keepdims=True)
    centred = resid - mean_row
    var_row = jnp.mean(centred * centred, axis=1, keepdims=True)
    scale_row = lax.rsqrt(var_row + eps_norm)
    normed = centred * scale_row
    return (normed * gain[None, :], normed, scale_row)


def norm_back(grad, normed, scale_row, gain):
    gain_grad = jnp.sum(grad * normed, axis=0)
    scaled = grad * gain[None, :]
    centre = jnp.mean(scaled, axis=1, keepdims=True)
    along = jnp.mean(scaled * normed, axis=1, keepdims=True)
    return (scale_row * (scaled - centre - normed * along), gain_grad)


def self_visible(query_side, key_side):
    same = query_side[0][:, None] == key_side[1][None, :]
    chosen = (key_side[0][None, :] == query_side[1][:, None]) | (
        key_side[2][None, :] < query_side[2][:, None]
    )
    return same & chosen


def cross_visible(query_side, key_side):
    return query_side[0][:, None] == key_side[1][None, :]


def block_scores(query, keys, visible):
    head_rows = query.shape[1] // HEAD_SIZE
    unscaled_scores = jnp.einsum(
        "qui,zui->uqz",
        query.reshape(query.shape[0], head_rows, HEAD_SIZE),
        keys.reshape(keys.shape[0], head_rows, HEAD_SIZE),
        preferred_element_type=jnp.float32,
    )
    return jnp.where(visible[None], unscaled_scores * (1.0 / math.sqrt(HEAD_SIZE)), neg_big)


def assemble(own_context, span, from_below, from_above):
    rows = own_context.shape[0]
    lower, upper = ([], [])
    count = min(rows, span)
    lower = [from_below(own_context[rows - count :], 1)] + lower
    upper = upper + [from_above(own_context[:count], 1)]
    return jnp.concatenate(lower + [own_context] + upper, axis=0)


def attend(query, keys, value_matrix, query_side, key_side, visible_fn):
    count = query.shape[0]
    head_rows = query.shape[1] // HEAD_SIZE
    scores = block_scores(query, keys, visible_fn(query_side, key_side))
    top = jnp.max(scores, axis=2)
    log_total = top + jnp.log(jnp.sum(jnp.exp(scores - top[:, :, None]), axis=2))
    probabilities = jnp.exp(scores - log_total[:, :, None])
    value_cube = value_matrix.reshape(value_matrix.shape[0], head_rows, HEAD_SIZE)
    out = jnp.einsum(
        "xiv,vxj->ixj",
        probabilities.astype(jnp.bfloat16),
        value_cube,
        preferred_element_type=jnp.float32,
    )
    return (out.reshape(count, head_rows * HEAD_SIZE).astype(jnp.bfloat16), log_total)


def attend_back(query, grad_low, log_total, keys, value_matrix, query_side, key_side, visible_fn):
    count = query.shape[0]
    model_width = keys.shape[0]
    head_rows = query.shape[1] // HEAD_SIZE
    scale_factor = 1.0 / math.sqrt(HEAD_SIZE)
    query_cube = query.reshape(count, head_rows, HEAD_SIZE)
    gradient_cube = grad_low.reshape(count, head_rows, HEAD_SIZE)
    key_cube = keys.reshape(model_width, head_rows, HEAD_SIZE)
    scores = block_scores(query, keys, visible_fn(query_side, key_side))
    probabilities = jnp.exp(scores - log_total[:, :, None])
    dprob = jnp.einsum(
        "qui,zui->uqz",
        gradient_cube,
        value_matrix.reshape(model_width, head_rows, HEAD_SIZE),
        preferred_element_type=jnp.float32,
    )
    delta = jnp.sum(probabilities * dprob, axis=2, keepdims=True)
    score_gradient = (probabilities * (dprob - delta)).astype(jnp.bfloat16)
    query_grad = (
        jnp.einsum("xiv,vxj->ixj", score_gradient, key_cube, preferred_element_type=jnp.float32)
        * scale_factor
    )
    key_rows = (
        jnp.einsum("exy,xei->yei", score_gradient, query_cube, preferred_element_type=jnp.float32)
        * scale_factor
    )
    value_rows = jnp.einsum(
        "exy,xei->yei",
        probabilities.astype(jnp.bfloat16),
        gradient_cube,
        preferred_element_type=jnp.float32,
    )
    return (
        query_grad.reshape(count, head_rows * HEAD_SIZE),
        key_rows.reshape(model_width, head_rows * HEAD_SIZE),
        value_rows.reshape(model_width, head_rows * HEAD_SIZE),
    )


def body(
    query_state,
    content,
    encoded,
    sentence_lengths,
    key_score,
    query_cut,
    w_query,
    w_key,
    w_value,
    w_out,
    gain_self,
    w_cross_query,
    w_cross_key,
    w_cross_value,
    w_cross_out,
    gain_cross,
    w_inner,
    w_outer,
    gain_final,
    out_grad,
):
    rows = query_state.shape[0]
    head_rows = w_query.shape[1] // HEAD_SIZE
    columns = head_rows * HEAD_SIZE
    total_rows = rows * lax.axis_size("seq")
    span = DOC_LEN - 1
    model_width = rows + 2 * span
    begin = lax.axis_index("seq") * rows
    own_pos = begin + jnp.arange(rows, dtype=jnp.int32)
    window_pos = begin - span + jnp.arange(model_width, dtype=jnp.int32)
    inside = (window_pos >= 0) & (window_pos < total_rows)
    own_sentence, own_first = sentence_of(own_pos, sentence_lengths)
    window_sentence = jnp.where(inside, sentence_of(window_pos, sentence_lengths)[0], -1)
    padded_score = jnp.pad(key_score, (span, span), constant_values=LEVELS)
    window_score = lax.dynamic_slice_in_dim(padded_score, begin, model_width, 0)
    own_cut = lax.dynamic_slice_in_dim(query_cut, begin, rows, 0)
    query_side = (own_sentence, own_first, own_cut)
    key_side = (window_pos, window_sentence, window_score)
    query = forward_product(query_state, w_query).astype(jnp.bfloat16)
    keys_own = forward_product(content, w_key).astype(jnp.bfloat16)
    values_own = forward_product(content, w_value).astype(jnp.bfloat16)
    cross_keys_own = forward_product(encoded, w_cross_key).astype(jnp.bfloat16)
    cross_values_own = forward_product(encoded, w_cross_value).astype(jnp.bfloat16)
    own_context = jnp.concatenate([keys_own, values_own, cross_keys_own, cross_values_own], axis=1)
    window = assemble(
        own_context,
        span,
        lambda piece, step: from_behind(piece, "seq", step),
        lambda piece, step: from_behind(piece, "seq", -step),
    )
    attn_low, lse_self = attend(
        query,
        window[:, :columns],
        window[:, columns : 2 * columns],
        query_side,
        key_side,
        self_visible,
    )
    branch_self = lax.psum(forward_product(attn_low, w_out), "head")
    hidden_one, normed_one, scale_one = layer_norm(
        query_state.astype(jnp.float32) + branch_self, gain_self
    )
    hidden_one_low = hidden_one.astype(jnp.bfloat16)
    cross_query = forward_product(hidden_one_low, w_cross_query).astype(jnp.bfloat16)
    cross_low, lse_cross = attend(
        cross_query,
        window[:, 2 * columns : 3 * columns],
        window[:, 3 * columns :],
        query_side,
        key_side,
        cross_visible,
    )
    branch_cross = lax.psum(forward_product(cross_low, w_cross_out), "head")
    hidden_two, normed_two, scale_two = layer_norm(hidden_one + branch_cross, gain_cross)
    hidden_two_low = hidden_two.astype(jnp.bfloat16)
    inner = forward_product(hidden_two_low, w_inner)
    active_low = jax.nn.gelu(inner, approximate=False).astype(jnp.bfloat16)
    branch_ffn = lax.psum(forward_product(active_low, w_outer), "head")
    mixed, normed_three, scale_three = layer_norm(hidden_two + branch_ffn, gain_final)
    window = assemble(
        own_context,
        span,
        lambda piece, step: from_behind(piece, "seq", step),
        lambda piece, step: from_behind(piece, "seq", -step),
    )
    grad_three, gain_final_grad = norm_back(
        out_grad.astype(jnp.float32), normed_three, scale_three, gain_final
    )
    ffn_low = grad_three.astype(jnp.bfloat16)
    outer_w_grad = rows_product(active_low, ffn_low)
    active_grad = weight_back(ffn_low, w_outer)
    gelu_back = jax.vjp(partial(jax.nn.gelu, approximate=False), inner)[1]
    inner_low = gelu_back(active_grad)[0].astype(jnp.bfloat16)
    inner_w_grad = rows_product(hidden_two_low, inner_low)
    grad_two = grad_three + lax.psum(weight_back(inner_low, w_inner), "head")
    resid_two_grad, gain_cross_grad = norm_back(grad_two, normed_two, scale_two, gain_cross)
    cross_branch_low = resid_two_grad.astype(jnp.bfloat16)
    cross_out_w_grad = rows_product(cross_low, cross_branch_low)
    cross_attn_grad = weight_back(cross_branch_low, w_cross_out).astype(jnp.bfloat16)
    cross_query_grad, cross_key_rows, cross_value_rows = attend_back(
        cross_query,
        cross_attn_grad,
        lse_cross,
        window[:, 2 * columns : 3 * columns],
        window[:, 3 * columns :],
        query_side,
        key_side,
        cross_visible,
    )
    cross_query_low = cross_query_grad.astype(jnp.bfloat16)
    cross_query_w_grad = rows_product(hidden_one_low, cross_query_low)
    grad_one = resid_two_grad + lax.psum(
        weight_back(cross_query_low, w_cross_query).astype(jnp.bfloat16), "head"
    ).astype(jnp.float32)
    resid_one_grad, gain_self_grad = norm_back(grad_one, normed_one, scale_one, gain_self)
    self_branch_low = resid_one_grad.astype(jnp.bfloat16)
    out_w_grad = rows_product(attn_low, self_branch_low)
    attn_grad = weight_back(self_branch_low, w_out).astype(jnp.bfloat16)
    query_grad, self_key_rows, self_value_rows = attend_back(
        query,
        attn_grad,
        lse_self,
        window[:, :columns],
        window[:, columns : 2 * columns],
        query_side,
        key_side,
        self_visible,
    )
    window_grads = jnp.concatenate(
        [self_key_rows, self_value_rows, cross_key_rows, cross_value_rows], axis=1
    )
    own_grads = window_grads[span : span + rows]
    step = 1
    count = min(rows, span - (step - 1) * rows)
    edge = span - (step - 1) * rows
    returned_low = from_behind(
        window_grads[edge - count : edge].astype(jnp.bfloat16), "seq", -step
    ).astype(jnp.float32)
    own_grads = own_grads + jnp.pad(returned_low, ((rows - count, 0), (0, 0)))
    start = span + step * rows
    returned_high = from_behind(
        window_grads[start : start + count].astype(jnp.bfloat16), "seq", step
    ).astype(jnp.float32)
    own_grads = own_grads + jnp.pad(returned_high, ((0, rows - count), (0, 0)))
    key_low = tuple(
        (own_grads[:, k * columns : (k + 1) * columns].astype(jnp.bfloat16) for k in range(4))
    )
    query_low = query_grad.astype(jnp.bfloat16)
    query_w_grad = rows_product(query_state, query_low)
    key_w_grad = rows_product(content, key_low[0])
    value_w_grad = rows_product(content, key_low[1])
    cross_key_w_grad = rows_product(encoded, key_low[2])
    cross_value_w_grad = rows_product(encoded, key_low[3])
    query_part = weight_back(query_low, w_query)
    content_part = weight_back(key_low[0], w_key) + weight_back(key_low[1], w_value)
    encoded_part = weight_back(key_low[2], w_cross_key) + weight_back(key_low[3], w_cross_value)
    query_sum, content_grad, encoded_grad = (
        lax.psum(query_part.astype(jnp.bfloat16), "head").astype(jnp.float32),
        lax.psum(content_part.astype(jnp.bfloat16), "head").astype(jnp.float32),
        lax.psum(encoded_part.astype(jnp.bfloat16), "head").astype(jnp.float32),
    )
    query_state_grad = resid_one_grad + query_sum
    summed = (
        lax.psum(query_w_grad.astype(jnp.bfloat16), "seq").astype(jnp.float32),
        lax.psum(key_w_grad.astype(jnp.bfloat16), "seq").astype(jnp.float32),
        lax.psum(value_w_grad.astype(jnp.bfloat16), "seq").astype(jnp.float32),
        lax.psum(out_w_grad.astype(jnp.bfloat16), "seq").astype(jnp.float32),
        lax.psum(gain_self_grad.astype(jnp.bfloat16), "seq").astype(jnp.float32),
        lax.psum(cross_query_w_grad.astype(jnp.bfloat16), "seq").astype(jnp.float32),
        lax.psum(cross_key_w_grad.astype(jnp.bfloat16), "seq").astype(jnp.float32),
        lax.psum(cross_value_w_grad.astype(jnp.bfloat16), "seq").astype(jnp.float32),
        lax.psum(cross_out_w_grad.astype(jnp.bfloat16), "seq").astype(jnp.float32),
        lax.psum(gain_cross_grad.astype(jnp.bfloat16), "seq").astype(jnp.float32),
        lax.psum(inner_w_grad.astype(jnp.bfloat16), "seq").astype(jnp.float32),
        lax.psum(outer_w_grad.astype(jnp.bfloat16), "seq").astype(jnp.float32),
        lax.psum(gain_final_grad.astype(jnp.bfloat16), "seq").astype(jnp.float32),
    )
    return (
        mixed.astype(jnp.bfloat16),
        query_state_grad,
        content_grad,
        encoded_grad,
        summed[0],
        summed[1],
        summed[2],
        summed[3],
        summed[4],
        summed[5],
        summed[6],
        summed[7],
        summed[8],
        summed[9],
        summed[10],
        summed[11],
        summed[12],
    )


def solution(mesh):
    in_specs = (
        P("seq", None),
        P("seq", None),
        P("seq", None),
        P(),
        P(),
        P(),
        P(None, "head"),
        P(None, "head"),
        P(None, "head"),
        P("head", None),
        P(),
        P(None, "head"),
        P(None, "head"),
        P(None, "head"),
        P("head", None),
        P(),
        P(None, "head"),
        P("head", None),
        P(),
        P("seq", None),
    )
    out_specs = (
        P("seq", None),
        P("seq", None),
        P("seq", None),
        P("seq", None),
        P(None, "head"),
        P(None, "head"),
        P(None, "head"),
        P("head", None),
        P(),
        P(None, "head"),
        P(None, "head"),
        P(None, "head"),
        P("head", None),
        P(),
        P(None, "head"),
        P("head", None),
        P(),
    )
    return jax.shard_map(body, mesh=mesh, in_specs=in_specs, out_specs=out_specs, check_vma=False)
```

profile of v0, /device:TPU:0, one launch (start us, length us, event | category | flops | bytes accessed | tf_op | source)
XLA Modules:
  0.0 1293.5 jit_solution(4653720718130799541)
XLA Ops:
  16.5 4.2 collective-permute-start
  23.0 10.3 broadcast_compare_fusion
  34.0 7.1 concatenate.11
  41.1 3.7 fusion.61
  45.3 17.2 %fusion = (f32[2,1536]{1,0:T(2,128)S(1)}, f32[2,1536,3582]{2,1,0:T(8,128)}) fusion(pred[1536,3582]{1,0:T(8,128)(4,1)S(1)} %copy-done.1, bf16[1536,2,64]{0,2,1:T(8,128)(2,1)S(1)} %bitcast.131, bf16[3582,2,64]{0,2,1:T(8,128)(2,1)S(1)} %bitcast.119), kind=kOutput, calls=%fused_computation.10 | convolution fusion | flops 1441508352 | bytes 50840064 | tf_op jit(solution)/shard_map/qui,zui->uqz/dot_general | solution.py:75
  62.5 20.4 %exponential_reduce_fusion.1 = f32[2,1536]{1,0:T(2,128)S(1)} fusion(f32[2,1536,3582]{2,1,0:T(8,128)} %get-tuple-element.117, f32[2,1536]{1,0:T(2,128)S(1)} %get-tuple-element.116, pred[1536,3582]{1,0:T(8,128)(4,1)S(1)} %copy-done.1), kind=kLoop, calls=%fused_computation.8 | loop fusion | flops 44012544 | bytes 49542144 | tf_op jit(solution)/shard_map/reduce_sum | solution.py:98
  83.0 19.9 %convolution_convert_fusion.6 = bf16[2,64,1536]{2,1,0:T(8,128)(2,1)} fusion(bf16[3582,2,64]{0,2,1:T(8,128)(2,1)S(1)} %bitcast.136, f32[2,1536,3582]{2,1,0:T(8,128)} %get-tuple-element.117, f32[2,1536]{1,0:T(2,128)S(1)} %log_add_fusion.1, pred[1536,3582]{1,0:T(8,128)(4,1)} %get-tuple-element.115), kind=kOutput, calls=%fused_computation.85 | convolution fusion | flops 1452711936 | bytes 50840064 | tf_op jit(solution)/shard_map/xiv,vxj->ixj/dot_general | solution.py:101
  106.4 132.4 %all-reduce.15.cloned.1.call-done = f32[1536,512]{1,0:T(8,128)} async-done(((f32[1536,512]{1,0:T(8,128)}), f32[1536,512]{1,0:T(8,128)}) %all-reduce.15.cloned.1.call-update) | async-done | bytes 3145744 | tf_op jit(solution)/shard_map/psum | solution.py:208
  245.4 17.1 %fusion.1 = (f32[2,1536]{1,0:T(2,128)S(1)}, f32[2,1536,3582]{2,1,0:T(8,128)}) fusion(pred[1536,3582]{1,0:T(8,128)(4,1)S(1)} %bitcast.114, bf16[1536,2,64]{0,2,1:T(8,128)(2,1)S(1)} %bitcast.133, bf16[3582,2,64]{0,2,1:T(8,128)(2,1)S(1)} %bitcast.121), kind=kOutput, calls=%fused_computation.11 | convolution fusion | flops 1441508352 | bytes 50840064 | tf_op jit(solution)/shard_map/qui,zui->uqz/dot_general | solution.py:75
  262.5 20.4 %exponential_reduce_fusion = f32[2,1536]{1,0:T(2,128)S(1)} fusion(f32[2,1536,3582]{2,1,0:T(8,128)} %get-tuple-element.119, f32[2,1536]{1,0:T(2,128)S(1)} %get-tuple-element.118, pred[1536,3582]{1,0:T(8,128)(4,1)S(1)} %bitcast.114), kind=kLoop, calls=%fused_computation.5 | loop fusion | flops 44012544 | bytes 49542144 | tf_op jit(solution)/shard_map/reduce_sum | solution.py:98
  282.9 19.1 %convolution_convert_fusion.4 = bf16[2,64,1536]{2,1,0:T(8,128)(2,1)S(1)} fusion(bf16[3582,2,64]{0,2,1:T(8,128)(2,1)S(1)} %bitcast.137, f32[2,1536,3582]{2,1,0:T(8,128)} %get-tuple-element.119, f32[2,1536]{1,0:T(2,128)S(1)} %log_add_fusion, pred[1536,3582]{1,0:T(8,128)(4,1)} %get-tuple-element.114), kind=kOutput, calls=%fused_computation.83 | convolution fusion | flops 1452711936 | bytes 50840064 | tf_op jit(solution)/shard_map/xiv,vxj->ixj/dot_general | solution.py:101
  304.8 119.8 %all-reduce.17.cloned.1.call-done = f32[1536,512]{1,0:T(8,128)} async-done(((f32[1536,512]{1,0:T(8,128)}), f32[1536,512]{1,0:T(8,128)}) %all-reduce.17.cloned.1.call-update) | async-done | bytes 3145744 | tf_op jit(solution)/shard_map/psum | solution.py:222
  430.2 8.6 multiply_convert_fusion.3
  442.9 120.2 %all-reduce.19.cloned.1.call-done = f32[1536,512]{1,0:T(8,128)} async-done(((f32[1536,512]{1,0:T(8,128)}), f32[1536,512]{1,0:T(8,128)}) %all-reduce.19.cloned.1.call-update) | async-done | bytes 3145744 | tf_op jit(solution)/shard_map/psum | solution.py:227
  585.6 113.2 %all-reduce.21.cloned.1.call-done = f32[1536,512]{1,0:T(8,128)} async-done(((f32[1536,512]{1,0:T(8,128)}), f32[1536,512]{1,0:T(8,128)}) %all-reduce.21.cloned.1.call-update) | async-done | bytes 3145744 | tf_op jit(solution)/shard_map/psum | solution.py:244
  698.9 5.6 multiply_reduce_fusion.2
  708.1 21.3 %fusion.49 = f32[2,64,3582]{2,1,0:T(8,128)} fusion(bf16[1536,2,64]{0,2,1:T(8,128)(2,1)S(1)} %bitcast.139, f32[2,1536,3582]{2,1,0:T(8,128)} %get-tuple-element.119, f32[2,1536]{1,0:T(2,128)S(1)} %log_add_fusion, pred[1536,3582]{1,0:T(8,128)(4,1)} %get-tuple-element.114), kind=kOutput, calls=%fused_computation.149 | convolution fusion | flops 1452515328 | bytes 51757056 | tf_op jit(solution)/shard_map/exy,xei->yei/dot_general | solution.py:136
  729.4 32.4 %multiply_reduce_fusion.1 = (f32[2,1536]{1,0:T(2,128)S(1)}, f32[2,1536,3582]{2,1,0:T(8,128)}) fusion(f32[2,1536,3582]{2,1,0:T(8,128)} %get-tuple-element.119, f32[2,1536]{1,0:T(2,128)S(1)} %log_add_fusion, pred[1536,3582]{1,0:T(8,128)(4,1)} %get-tuple-element.114, bf16[1536,2,64]{0,2,1:T(8,128)(2,1)S(1)} %bitcast.140, bf16[3582,2,64]{0,2,1:T(8,128)(2,1)S(1)} %bitcast.138), kind=kOutput, calls=%fused_computation.3 | convolution fusion | flops 1463516160 | bytes 94867968 | tf_op jit(solution)/shard_map/qui,zui->uqz/dot_general | solution.py:120
  761.8 37.0 %multiply_convert_fusion.1 = bf16[2,1536,3582]{2,1,0:T(8,128)(2,1)} fusion(f32[2,1536,3582]{2,1,0:T(8,128)} %get-tuple-element.122, f32[2,1536,3582]{2,1,0:T(8,128)} %get-tuple-element.119, f32[2,1536]{1,0:T(2,128)S(1)} %get-tuple-element.121, f32[2,1536]{1,0:T(2,128)S(1)} %log_add_fusion, pred[1536,3582]{1,0:T(8,128)(4,1)} %get-tuple-element.114), kind=kLoop, calls=%fused_computation.2 | loop fusion | flops 66023424 | bytes 115565568 | tf_op jit(solution)/shard_map/convert_element_type | solution.py:127
  798.8 11.4 fusion.21
  816.4 9.4 convolution_multiply_fusion
  825.8 54.5 %all-reduce.23.cloned.1.call-done = bf16[1536,512]{1,0:T(8,128)(2,1)} async-done(((bf16[1536,512]{1,0:T(8,128)(2,1)}), bf16[1536,512]{1,0:T(8,128)(2,1)}) %all-reduce.23.cloned.1.call-update) | async-done | bytes 1572880 | tf_op jit(solution)/shard_map/psum | solution.py:261
  880.3 4.2 multiply_reduce_fusion.3
  890.3 21.2 %fusion.52 = f32[2,64,3582]{2,1,0:T(8,128)} fusion(bf16[1536,2,64]{0,2,1:T(8,128)(2,1)S(1)} %bitcast.141, f32[2,1536,3582]{2,1,0:T(8,128)} %get-tuple-element.117, f32[2,1536]{1,0:T(2,128)S(1)} %copy-done.63, pred[1536,3582]{1,0:T(8,128)(4,1)} %get-tuple-element.115), kind=kOutput, calls=%fused_computation.150 | convolution fusion | flops 1452515328 | bytes 51757056 | tf_op jit(solution)/shard_map/exy,xei->yei/dot_general | solution.py:136
  911.5 32.8 %multiply_reduce_fusion = (f32[2,1536]{1,0:T(2,128)S(1)}, f32[2,1536,3582]{2,1,0:T(8,128)}) fusion(f32[2,1536,3582]{2,1,0:T(8,128)} %get-tuple-element.117, f32[2,1536]{1,0:T(2,128)S(1)} %copy-done.63, pred[1536,3582]{1,0:T(8,128)(4,1)} %get-tuple-element.115, bf16[1536,2,64]{0,2,1:T(8,128)(2,1)} %bitcast.142, bf16[3582,2,64]{0,2,1:T(8,128)(2,1)} %bitcast.135), kind=kOutput, calls=%fused_computation.1 | convolution fusion | flops 1463516160 | bytes 94867968 | tf_op jit(solution)/shard_map/qui,zui->uqz/dot_general | solution.py:120
  944.3 37.0 %multiply_convert_fusion = bf16[2,1536,3582]{2,1,0:T(8,128)(2,1)} fusion(f32[2,1536,3582]{2,1,0:T(8,128)} %get-tuple-element.124, f32[2,1536,3582]{2,1,0:T(8,128)} %get-tuple-element.117, f32[2,1536]{1,0:T(2,128)S(1)} %get-tuple-element.123, f32[2,1536]{1,0:T(2,128)S(1)} %copy-done.63, pred[1536,3582]{1,0:T(8,128)(4,1)} %get-tuple-element.115), kind=kLoop, calls=%fused_computation | loop fusion | flops 66023424 | bytes 115565568 | tf_op jit(solution)/shard_map/convert_element_type | solution.py:127
  981.3 11.3 fusion.22
  992.7 9.5 convolution_multiply_fusion.1
  1024.5 30.1 %all-reduce.4 = (bf16[512]{0:T(512)(128)(2,1)S(1)}, bf16[512]{0:T(512)(128)(2,1)S(1)}, bf16[512]{0:T(512)(128)(2,1)S(1)}) all-reduce(bf16[512]{0:T(512)(128)(2,1)S(1)} %get-tuple-element.68, bf16[512]{0:T(512)(128)(2,1)S(1)} %copy-done.70, bf16[512]{0:T(512)(128)(2,1)S(1)} %copy-done.69), channel_id=1, replica_groups=mesh['seq'=8,'head'=4] {'seq'}, use_global_device_ids=true, to_apply=%region_36.37 | all-reduce | flops 1536 | bytes 6144 | tf_op jit(solution)/shard_map/psum | solution.py:317
  1056.4 45.9 %all-reduce.25.cloned.1.call-done = (bf16[512,128]{0,1:T(8,128)(2,1)}, bf16[512,128]{0,1:T(8,128)(2,1)}, bf16[512,128]{0,1:T(8,128)(2,1)}, bf16[512,128]{0,1:T(8...) async-done(((bf16[512,128]{0,1:T(8,128)(2,1)}, ...) | async-done | bytes 2097168 | tf_op jit(solution)/shard_map/psum | solution.py:313
  1118.1 159.5 %all-reduce.27.cloned.1.call-done = (bf16[1536,512]{1,0:T(8,128)(2,1)}, bf16[1536,512]{1,0:T(8,128)(2,1)}, bf16[1536,512]{1,0:T(8,128)(2,1)}) async-done(((bf16[1536,512]{1,0:T(8,128)(2,1)}, bf16[1536,512]{1,0:T(8,128)(2,1)}, bf16[1536,512]{1,0:T(8,128)(2,1)}), (bf16[1536,512]{1,0:T(8,128)(2,1)}, bf16[1536,512]{1,0:T(8,128)(2,1)}, bf16[1536,512]{1,0:T(8,128)(2,1)})) %all-reduce.27.cloned.1.call-update) | async-done | bytes 4718608 | tf_op jit(solution)/shard_map/psum | solution.py:307
  1277.6 4.6 convert_add_fusion
  (262 shorter events, 116.8 us)
Async XLA Ops:
  7.2 231.6 %all-reduce.15.cloned.1.call-start = ((), (), s32[]{:S(2)}) async-start(), calls=%async_computation | async-start | bytes 6291456 | tf_op jit(solution)/shard_map/psum | solution.py:208
  15.2 18.7 %collective-permute-start.1 = (bf16[1023,512]{0,1:T(8,128)(2,1)}, bf16[1023,512]{0,1:T(8,128)(2,1)}, u32[]{:S(2)}, u32[]{:S(2)}) collective-permute-start(bf16[1023,512]{0,1:T(8,128)(2,1)} %get-tuple-element.112), channel_id=1, source_target_pairs={{4,0},{8,4},{12,8},{16,12},{20,16},{24,20},{28,24},{5,1},{9,5},{13... | collective-permute-start | bytes 3142664 | tf_op jit(solution)/shard_map/ppermute | solution.py:21
  16.5 17.4 %collective-permute-start = (bf16[1023,512]{0,1:T(8,128)(2,1)}, bf16[1023,512]{0,1:T(8,128)(2,1)}, u32[]{:S(2)}, u32[]{:S(2)}) collective-permute-start(bf16[1023,512]{0,1:T(8,128)(2,1)} %get-tuple-element.113), channel_id=1, source_target_pairs={{0,4},{4,8},{8,12},{12,16},{16,20},{20,24},{24,28},{1,5},{5,9},{9,... | collective-permute-start | bytes 3142664 | tf_op jit(solution)/shard_map/ppermute | solution.py:21
  33.9 10.8 copy-start.27
  44.8 17.7 %copy-start.12 = (bf16[3582,128]{0,1:T(8,128)(2,1)}, bf16[3582,128]{0,1:T(8,128)(2,1)S(1)}, u32[]{:S(2)}) copy-start(bf16[3582,128]{0,1:T(8,128)(2,1)S(1)} %get-tuple-element.108) | copy-start | bytes 2750980
  44.8 200.6 %copy-start.13 = (bf16[3582,128]{0,1:T(8,128)(2,1)}, bf16[3582,128]{0,1:T(8,128)(2,1)S(1)}, u32[]{:S(2)}) copy-start(bf16[3582,128]{0,1:T(8,128)(2,1)S(1)} %get-tuple-element.106) | copy-start | bytes 2750980
  62.5 20.5 %copy-start.31 = (bf16[3582,128]{0,1:T(8,128)(2,1)S(1)}, bf16[3582,128]{0,1:T(8,128)(2,1)}, u32[]{:S(2)}) copy-start(bf16[3582,128]{0,1:T(8,128)(2,1)} %get-tuple-element.109) | copy-start | bytes 2750980
  82.9 19.9 %copy-start.62 = (f32[2,1536]{1,0:T(2,128)}, f32[2,1536]{1,0:T(2,128)S(1)}, u32[]{:S(2)}) copy-start(f32[2,1536]{1,0:T(2,128)S(1)} %log_add_fusion.1) | copy-start | bytes 36868
  83.0 19.9 %copy-start.48 = (bf16[128,512]{1,0:T(8,128)(2,1)S(1)}, bf16[128,512]{1,0:T(8,128)(2,1)}, u32[]{:S(2)}) copy-start(bf16[128,512]{1,0:T(8,128)(2,1)} %param.29) | copy-start | bytes 393220
  106.1 318.5 %all-reduce.17.cloned.1.call-start = ((), (), s32[]{:S(2)}) async-start(), calls=%async_computation.1 | async-start | bytes 6291456 | tf_op jit(solution)/shard_map/psum | solution.py:222
  241.8 182.9 %copy-start.58 = (f32[1536]{0:T(1024)}, f32[1536]{0:T(1024)S(1)}, u32[]{:S(2)}) copy-start(f32[1536]{0:T(1024)S(1)} %broadcast_multiply_fusion.8) | copy-start | bytes 18436
  242.4 182.2 %copy-start.60 = (f32[1536]{0:T(1024)}, f32[1536]{0:T(1024)S(1)}, u32[]{:S(2)}) copy-start(f32[1536]{0:T(1024)S(1)} %add_rsqrt_fusion.2) | copy-start | bytes 18436
  245.3 17.1 %copy-start.29 = (bf16[1536,128]{0,1:T(8,128)(2,1)}, bf16[1536,128]{0,1:T(8,128)(2,1)S(1)}, u32[]{:S(2)}) copy-start(bf16[1536,128]{0,1:T(8,128)(2,1)S(1)} %convolution_convert_fusion.5) | copy-start | bytes 1179652
  262.5 20.4 %copy-start.32 = (bf16[3582,128]{0,1:T(8,128)(2,1)S(1)}, bf16[3582,128]{0,1:T(8,128)(2,1)}, u32[]{:S(2)}) copy-start(bf16[3582,128]{0,1:T(8,128)(2,1)} %get-tuple-element.107) | copy-start | bytes 2750980
  282.9 19.1 %copy-start.45 = (bf16[128,512]{1,0:T(8,128)(2,1)S(1)}, bf16[128,512]{1,0:T(8,128)(2,1)}, u32[]{:S(2)}) copy-start(bf16[128,512]{1,0:T(8,128)(2,1)} %param.34) | copy-start | bytes 393220
  304.4 258.7 %all-reduce.19.cloned.1.call-start = ((), (), s32[]{:S(2)}) async-start(), calls=%async_computation.2 | async-start | bytes 6291456 | tf_op jit(solution)/shard_map/psum | solution.py:227
  442.8 256.0 %all-reduce.21.cloned.1.call-start = ((), (), s32[]{:S(2)}) async-start(), calls=%async_computation.3 | async-start | bytes 6291456 | tf_op jit(solution)/shard_map/psum | solution.py:244
  578.6 301.7 %all-reduce.23.cloned.1.call-start = ((), (), s32[]{:S(2)}) async-start(), calls=%async_computation.4 | async-start | bytes 3145728 | tf_op jit(solution)/shard_map/psum | solution.py:261
  708.1 21.3 %copy-start.33 = (bf16[3582,128]{0,1:T(8,128)(2,1)S(1)}, bf16[3582,128]{0,1:T(8,128)(2,1)}, u32[]{:S(2)}) copy-start(bf16[3582,128]{0,1:T(8,128)(2,1)} %get-tuple-element.107) | copy-start | bytes 2750980
  761.8 37.0 %copy-start.14 = (bf16[3582,128]{0,1:T(8,128)(2,1)S(1)}, bf16[3582,128]{0,1:T(8,128)(2,1)}, u32[]{:S(2)}) copy-start(bf16[3582,128]{0,1:T(8,128)(2,1)} %copy-done.13) | copy-start | bytes 2750980
  798.8 11.5 copy-start.47
  812.0 290.3 %all-reduce.25.cloned.1.call-start = ((), (), s32[]{:S(2)}) async-start(), calls=%async_computation.5 | async-start | bytes 4194304 | tf_op jit(solution)/shard_map/psum | solution.py:313
  816.4 63.9 %copy-start.59 = (f32[1536]{0:T(1024)S(1)}, f32[1536]{0:T(1024)}, u32[]{:S(2)}) copy-start(f32[1536]{0:T(1024)} %copy-done.58) | copy-start | bytes 18436
  816.4 63.9 %copy-start.61 = (f32[1536]{0:T(1024)S(1)}, f32[1536]{0:T(1024)}, u32[]{:S(2)}) copy-start(f32[1536]{0:T(1024)} %copy-done.60) | copy-start | bytes 18436
  816.4 63.9 %copy-start.66 = (f32[512]{0:T(512)S(1)}, f32[512]{0:T(512)}, u32[]{:S(2)}) copy-start(f32[512]{0:T(512)} %param.30) | copy-start | bytes 6148
  981.3 11.3 copy-start.28
  992.7 10.5 copy-start.22
  1005.3 8.0 collective-permute-start.2
  1006.7 6.6 collective-permute-start.3
  1018.8 258.8 %all-reduce.27.cloned.1.call-start = ((), (), s32[]{:S(2)}) async-start(), calls=%async_computation.6 | async-start | bytes 9437184 | tf_op jit(solution)/shard_map/psum | solution.py:307
  1102.3 13.6 %copy-start.44 = (bf16[512,512]{1,0:T(8,128)(2,1)S(1)}, bf16[512,512]{1,0:T(8,128)(2,1)}, u32[]{:S(2)}) copy-start(bf16[512,512]{1,0:T(8,128)(2,1)} %get-tuple-element.90) | copy-start | bytes 1572868
  1102.3 14.7 %copy-start.43 = (bf16[512,512]{1,0:T(8,128)(2,1)S(1)}, bf16[512,512]{1,0:T(8,128)(2,1)}, u32[]{:S(2)}) copy-start(bf16[512,512]{1,0:T(8,128)(2,1)} %get-tuple-element.91) | copy-start | bytes 1572868
  (55 other events, 200.1 us)
Sparse Core Ops, SparseCore 0:
  106.3 132.5 all-reduce.14
  304.5 120.0 all-reduce.16
  443.0 120.0 all-reduce.18
  578.7 120.0 all-reduce.20
  812.1 68.1 all-reduce.22
  1018.9 83.3 all-reduce.24
  1105.5 172.1 all-reduce.26
where the time goes:
time: 1300 us; the launch traced here: 1290 us
  waiting for transfers between devices  746 us (57%)
  matrix products  277 us (21%)
  other arithmetic  177 us (14%)
  local copies, waits for them, and re-layouts  37.6 us (3%)
  blocking collectives  30.1 us (2%)
  between operations  15.3 us (1%)
    psum x1, waiting for transfers between devices, body(): lax.psum(query_part.astype(jnp.bfloat16), 'head').astype(jnp.float32)  160 us
    psum x1, waiting for transfers between devices, body(): branch_self = lax.psum(forward_product(attn_low, w_out), 'head')  132 us
    psum x1, waiting for transfers between devices, body(): branch_ffn = lax.psum(forward_product(active_low, w_outer), 'head')  120 us
    psum x1, waiting for transfers between devices, body(): branch_cross = lax.psum(forward_product(cross_low, w_cross_out), 'head')  120 us
    psum x1, waiting for transfers between devices, body(): grad_two = grad_three + lax.psum(weight_back(inner_low, w_inner), 'head')  113 us
    convert_element_type x2, other arithmetic, attend_back(): score_gradient = (probabilities * (dprob - delta)).astype(jnp.bfloat16)  74 us
    dot_general x2, matrix products, attend_back(): jnp.einsum('qui,zui->uqz', gradient_cube, value_matrix.reshape(model_widt...  65.2 us
    psum x1, waiting for transfers between devices, body(): lax.psum(weight_back(cross_query_low, w_cross_query).astype(jnp.bfloat16)...  54.5 us
  transfers between devices with their start and end apart: 11, of which 7 were waited for; matrix products, arithmetic and copies ran while one was open for 5% of the time, Pallas kernels for 0%

commit v1 on v0

v1 whole, which is shorter than its diff:
```python
from functools import partial
import math

import jax
import jax.numpy as jnp
from jax import lax
from jax.experimental import pallas as pl
from jax.experimental.pallas import tpu as pltpu
from jax.sharding import PartitionSpec as P

HEADS = 8
HEAD_SIZE = 64
PAIR = 2 * HEAD_SIZE
PAIRS = HEADS // 2
DOC_LEN = 1024
CHUNK = 256
EPS = 1e-05
NEG_BIG = -1e30
LOG2E = 1.4426950408889634
SCALE = 1.0 / math.sqrt(HEAD_SIZE)
SCORE_SCALE = SCALE * LOG2E
CODES = 128
BF16 = jnp.bfloat16
F32 = jnp.float32
VMEM_LIMIT = 60 << 20


def dot_nn(left, right):
    return lax.dot_general(left, right, (((1,), (0,)), ((), ())), preferred_element_type=F32)


def dot_nt(left, right):
    return lax.dot_general(left, right, (((1,), (1,)), ((), ())), preferred_element_type=F32)


def dot_tn(left, right):
    return lax.dot_general(left, right, (((0,), (0,)), ((), ())), preferred_element_type=F32)


def chunk_rows(c):
    return pl.ds(pl.multiple_of(c * CHUNK, CHUNK), CHUNK)


def layer_norm(resid):
    mean_row = jnp.mean(resid, axis=1, keepdims=True)
    centred = resid - mean_row
    var_row = jnp.mean(centred * centred, axis=1, keepdims=True)
    scale_row = lax.rsqrt(var_row + EPS)
    return centred * scale_row, scale_row


def norm_back(grad, normed, scale_row, gain):
    gain_grad = jnp.sum(grad * normed, axis=0, keepdims=True)
    scaled = grad * gain
    centre = jnp.mean(scaled, axis=1, keepdims=True)
    along = jnp.mean(scaled * normed, axis=1, keepdims=True)
    return scale_row * (scaled - centre - normed * along), gain_grad


def spread_heads(source, target):
    target[...] = jnp.zeros_like(target)
    for h in range(HEADS):
        row = h * PAIR + (h % 2) * HEAD_SIZE
        target[row : row + HEAD_SIZE, :] = source[h * HEAD_SIZE : (h + 1) * HEAD_SIZE, :]


def pair_rows(source, p, target):
    rows = source.shape[0]
    both = source[:, p * PAIR : (p + 1) * PAIR]
    lane = lax.broadcasted_iota(jnp.int32, both.shape, 1)
    zero = jnp.zeros_like(both)
    target[p, 0:rows, :] = jnp.where(lane < HEAD_SIZE, both, zero)
    target[p, rows : 2 * rows, :] = jnp.where(lane < HEAD_SIZE, zero, both)


def mask_bias(code, low, high):
    return jnp.where((code >= low) & (code < high), 0.0, NEG_BIG).astype(F32)


def attend(bounds, window, code, low, high, w_key_t, w_value_t, spread, bias, top, total, out):
    top[...] = jnp.full_like(top, NEG_BIG)
    total[...] = jnp.zeros_like(total)
    out[...] = jnp.zeros_like(out)

    def step(c, carry):
        rows = window[chunk_rows(c), :]
        keys = dot_nt(rows, w_key_t[...]).astype(BF16)
        values_t = dot_nt(w_value_t[...], rows).astype(BF16)
        bias[...] = mask_bias(code[chunk_rows(c), :], low[...], high[...])
        for h in range(HEADS):
            p = h // 2
            scores = dot_nn(keys[:, p * PAIR : (p + 1) * PAIR], spread[h * PAIR : (h + 1) * PAIR, :])
            scores = scores * SCORE_SCALE + bias[...]
            before = top[h : h + 1, :]
            now = jnp.maximum(before, jnp.max(scores, axis=0, keepdims=True))
            weights = jnp.exp2(scores - now)
            shrink = jnp.exp2(before - now)
            top[h : h + 1, :] = now
            total[h : h + 1, :] = total[h : h + 1, :] * shrink + jnp.sum(weights, axis=0, keepdims=True)
            head = slice(h * HEAD_SIZE, (h + 1) * HEAD_SIZE)
            out[head, :] = out[head, :] * shrink + dot_nn(values_t[head, :], weights.astype(BF16))
        return carry

    lax.fori_loop(bounds[0], bounds[1], step, 0)
    for h in range(HEADS):
        head = slice(h * HEAD_SIZE, (h + 1) * HEAD_SIZE)
        out[head, :] = out[head, :] / total[h : h + 1, :]


def attend_back(
    bounds, window, code, low, high, w_key_t, w_value_t, spread, grad_spread, pairs, grad_pairs, lse, delta, bias,
    query_grad, window_grad, w_key_grad, w_value_grad,
):
    chunks = window.shape[0] // CHUNK
    count = spread.shape[1]
    query_grad[...] = jnp.zeros_like(query_grad)
    w_key_grad[...] = jnp.zeros_like(w_key_grad)
    w_value_grad[...] = jnp.zeros_like(w_value_grad)

    def clear(c, carry):
        window_grad[chunk_rows(c), :] = jnp.zeros((CHUNK, window_grad.shape[1]), window_grad.dtype)
        return carry

    lax.fori_loop(0, bounds[0], clear, 0)
    lax.fori_loop(bounds[1], chunks, clear, 0)

    def step(c, carry):
        rows = window[chunk_rows(c), :]
        keys = dot_nt(rows, w_key_t[...]).astype(BF16)
        keys_t = dot_nt(w_key_t[...], rows).astype(BF16)
        values = dot_nt(rows, w_value_t[...]).astype(BF16)
        bias[...] = mask_bias(code[chunk_rows(c), :], low[...], high[...])
        key_grads, value_grads = [], []
        for p in range(PAIRS):
            columns = slice(p * PAIR, (p + 1) * PAIR)
            probs, score_grads = [], []
            for h in (2 * p, 2 * p + 1):
                wide = slice(h * PAIR, (h + 1) * PAIR)
                head = slice(h * HEAD_SIZE, (h + 1) * HEAD_SIZE)
                scores = dot_nn(keys[:, columns], spread[wide, :])
                prob = jnp.exp2(scores * SCORE_SCALE + bias[...] - lse[h : h + 1, :])
                dprob = dot_nn(values[:, columns], grad_spread[wide, :])
                score_grad = (prob * (dprob - delta[h : h + 1, :])).astype(BF16)
                query_grad[head, :] += dot_nn(keys_t[head, :], score_grad)
                probs.append(prob.astype(BF16))
                score_grads.append(score_grad)
            if count % 128 == 0:
                key_grads.append(dot_nn(jnp.concatenate(score_grads, axis=1), pairs[p]))
                value_grads.append(dot_nn(jnp.concatenate(probs, axis=1), grad_pairs[p]))
            else:
                key_grads.append(dot_nn(score_grads[0], pairs[p, 0:count]) + dot_nn(score_grads[1], pairs[p, count:]))
                value_grads.append(dot_nn(probs[0], grad_pairs[p, 0:count]) + dot_nn(probs[1], grad_pairs[p, count:]))
        keys_low = (jnp.concatenate(key_grads, axis=1) * SCALE).astype(BF16)
        values_low = jnp.concatenate(value_grads, axis=1).astype(BF16)
        window_grad[chunk_rows(c), :] = (
            dot_nn(keys_low, w_key_t[...]) + dot_nn(values_low, w_value_t[...])
        ).astype(window_grad.dtype)
        w_key_grad[...] += dot_tn(rows, keys_low)
        w_value_grad[...] += dot_tn(rows, values_low)
        return carry

    lax.fori_loop(bounds[0], bounds[1], step, 0)


def self_kernel(bounds, own, window, code, low, high, w_query_t, w_key_t, w_value_t, out, lse, spread, bias, top, total, low_t):
    low_t[...] = dot_nt(w_query_t[...], own[...]).astype(BF16)
    spread_heads(low_t, spread)
    attend(bounds, window, code, low, high, w_key_t, w_value_t, spread, bias, top, total, out)
    lse[...] = top[...] + jnp.log2(total[...])


def cross_kernel(
    bounds, own, attn_t, w_out, gain, window, code, low, high, w_query_t, w_key_t, w_value_t,
    hidden, out, lse, spread, bias, top, total, low_t,
):
    branch = dot_tn(attn_t[...].astype(BF16), w_out[...])
    normed, _ = layer_norm(own[...].astype(F32) + branch)
    hidden[...] = normed * gain[...]
    low_t[...] = dot_nt(w_query_t[...], hidden[...].astype(BF16)).astype(BF16)
    spread_heads(low_t, spread)
    attend(bounds, window, code, low, high, w_key_t, w_value_t, spread, bias, top, total, out)
    lse[...] = top[...] + jnp.log2(total[...])


def ffn_kernel(
    hidden_one, cross_t, w_out, gain_cross, w_inner, w_outer, gain_final, out_grad,
    mixed, resid_grad, w_out_grad, w_inner_grad, w_outer_grad, gain_cross_grad, gain_final_grad,
    normed_two, hidden_two_low, slope, active, sum_ffn,
):
    slices = w_inner.shape[0]
    cross_low = cross_t[...].astype(BF16)
    normed, scale_two = layer_norm(hidden_one[...] + dot_tn(cross_low, w_out[...]))
    normed_two[...] = normed
    hidden_two = normed * gain_cross[...]
    hidden_two_low[...] = hidden_two.astype(BF16)
    sum_ffn[...] = hidden_two
    for z in range(slices):
        inner = dot_nn(hidden_two_low[...], w_inner[z])
        below = 0.5 * (1.0 + lax.erf(inner * math.sqrt(0.5)))
        slope[z] = below + inner * (jnp.exp2(inner * inner * (-0.5 * LOG2E)) * (1.0 / math.sqrt(2.0 * math.pi)))
        active[z] = (inner * below).astype(BF16)
        sum_ffn[...] += dot_nn(active[z], w_outer[z])
    normed_three, scale_three = layer_norm(sum_ffn[...])
    mixed[...] = (normed_three * gain_final[...]).astype(BF16)
    grad_three, gain_grad = norm_back(out_grad[...].astype(F32), normed_three, scale_three, gain_final[...])
    gain_final_grad[...] = gain_grad
    ffn_low = grad_three.astype(BF16)
    sum_ffn[...] = grad_three
    for z in range(slices):
        w_outer_grad[z] = dot_tn(active[z], ffn_low).astype(BF16)
        inner_low = (dot_nt(ffn_low, w_outer[z]) * slope[z]).astype(BF16)
        w_inner_grad[z] = dot_tn(hidden_two_low[...], inner_low).astype(BF16)
        sum_ffn[...] += dot_nt(inner_low, w_inner[z])
    grad, gain_grad = norm_back(sum_ffn[...], normed_two[...], scale_two, gain_cross[...])
    gain_cross_grad[...] = gain_grad
    resid_grad[...] = grad
    w_out_grad[...] = dot_nn(cross_low, grad.astype(BF16)).astype(BF16)


def prepare_back(query, query_t, grad, grad_t, out, spread, grad_spread, pairs, grad_pairs, delta, low_t):
    low_t[...] = query_t.astype(BF16)
    spread_heads(low_t, spread)
    for p in range(PAIRS):
        pair_rows(query.astype(BF16), p, pairs)
        pair_rows(grad.astype(BF16), p, grad_pairs)
    low_t[...] = grad_t.astype(BF16)
    spread_heads(low_t, grad_spread)
    for h in range(HEADS):
        head = slice(h * HEAD_SIZE, (h + 1) * HEAD_SIZE)
        delta[h : h + 1, :] = jnp.sum(low_t[head, :].astype(F32) * out[head, :], axis=0, keepdims=True)


def cross_back_kernel(
    bounds, own, self_t, w_out, gain, resid_two_grad, w_cross_out, cross_t, lse, window, code, low, high,
    w_query_t, w_key_t, w_value_t,
    resid_one_grad, window_grad, w_query_grad, w_key_grad, w_value_grad, w_out_grad, gain_grad,
    spread, grad_spread, pairs, grad_pairs, delta, bias, low_t, query_grad, key_sum, value_sum, normed_one, scale_one,
):
    self_low = self_t[...].astype(BF16)
    normed, scale = layer_norm(own[...].astype(F32) + dot_tn(self_low, w_out[...]))
    normed_one[...] = normed
    scale_one[...] = scale
    hidden_low = (normed * gain[...]).astype(BF16)
    branch_low = resid_two_grad[...].astype(BF16)
    prepare_back(
        dot_nt(hidden_low, w_query_t[...]), dot_nt(w_query_t[...], hidden_low),
        dot_nt(branch_low, w_cross_out[...]), dot_nt(w_cross_out[...], branch_low),
        cross_t, spread, grad_spread, pairs, grad_pairs, delta, low_t,
    )
    attend_back(
        bounds, window, code, low, high, w_key_t, w_value_t, spread, grad_spread, pairs, grad_pairs, lse, delta, bias,
        query_grad, window_grad, key_sum, value_sum,
    )
    w_key_grad[...] = key_sum[...].astype(BF16)
    w_value_grad[...] = value_sum[...].astype(BF16)
    query_low = (query_grad[...] * SCALE).astype(BF16)
    hidden_low = (normed_one[...] * gain[...]).astype(BF16)
    w_query_grad[...] = dot_nn(query_low, hidden_low).astype(BF16)
    grad_one = resid_two_grad[...] + dot_tn(query_low, w_query_t[...])
    grad, gain_sum = norm_back(grad_one, normed_one[...], scale_one[...], gain[...])
    gain_grad[...] = gain_sum
    resid_one_grad[...] = grad
    w_out_grad[...] = dot_nn(self_t[...].astype(BF16), grad.astype(BF16)).astype(BF16)


def self_back_kernel(
    bounds, own, resid_one_grad, w_out, self_t, lse, window, code, low, high, w_query_t, w_key_t, w_value_t,
    own_grad, window_grad, w_query_grad, w_key_grad, w_value_grad,
    spread, grad_spread, pairs, grad_pairs, delta, bias, low_t, query_grad, key_sum, value_sum,
):
    branch_low = resid_one_grad[...].astype(BF16)
    prepare_back(
        dot_nt(own[...], w_query_t[...]), dot_nt(w_query_t[...], own[...]),
        dot_nt(branch_low, w_out[...]), dot_nt(w_out[...], branch_low),
        self_t, spread, grad_spread, pairs, grad_pairs, delta, low_t,
    )
    attend_back(
        bounds, window, code, low, high, w_key_t, w_value_t, spread, grad_spread, pairs, grad_pairs, lse, delta, bias,
        query_grad, window_grad, key_sum, value_sum,
    )
    w_key_grad[...] = key_sum[...].astype(BF16)
    w_value_grad[...] = value_sum[...].astype(BF16)
    query_low = (query_grad[...] * SCALE).astype(BF16)
    w_query_grad[...] = dot_nn(query_low, own[...]).astype(BF16)
    own_grad[...] = (resid_one_grad[...] + dot_tn(query_low, w_query_t[...])).astype(BF16)


def call(kernel, outs, scratch, smem, *args):
    place = [pl.BlockSpec(memory_space=pltpu.SMEM)] * smem
    place += [pl.BlockSpec(memory_space=pltpu.VMEM)] * (len(args) - smem)
    return pl.pallas_call(
        kernel,
        out_shape=[jax.ShapeDtypeStruct(shape, kind) for shape, kind in outs],
        in_specs=place,
        out_specs=[pl.BlockSpec(memory_space=pltpu.VMEM)] * len(outs),
        scratch_shapes=[pltpu.VMEM(shape, kind) for shape, kind in scratch],
        compiler_params=pltpu.CompilerParams(vmem_limit_bytes=VMEM_LIMIT),
    )(*args)


def shifted(value, by):
    peers = lax.axis_size("seq")
    return lax.ppermute(value, "seq", [(i, i + by) for i in range(peers) if 0 <= i + by < peers])


def body(
    query_state, content, encoded, sentence_lengths, key_score, query_cut, w_query, w_key, w_value, w_out, gain_self,
    w_cross_query, w_cross_key, w_cross_value, w_cross_out, gain_cross, w_inner, w_outer, gain_final, out_grad,
):
    rows, width = query_state.shape
    slices = lax.axis_size("head")
    count = rows // slices
    wide = -(-(count + 2 * DOC_LEN) // CHUNK) * CHUNK
    spare = wide - count - 2 * DOC_LEN
    total_rows = rows * lax.axis_size("seq")
    seq, part = lax.axis_index("seq"), lax.axis_index("head")
    begin = seq * rows + part * count
    window_pos = begin - DOC_LEN + jnp.arange(wide, dtype=jnp.int32)

    ends = jnp.cumsum(sentence_lengths)
    passed = (window_pos[:, None] >= ends[None, :]).astype(jnp.int32)
    sentence = jnp.sum(passed, axis=1)
    first = jnp.sum(passed * sentence_lengths[None, :], axis=1)
    inside = (window_pos >= 0) & (window_pos < total_rows)
    score = lax.dynamic_slice_in_dim(jnp.pad(key_score, (DOC_LEN, DOC_LEN + spare)), begin, wide, 0)
    score = jnp.where(window_pos == first, -1, score)
    code = jnp.where(inside, sentence * CODES + score, -CODES).reshape(wide, 1)
    own_sentence = lax.slice_in_dim(sentence, DOC_LEN, DOC_LEN + count)
    own_cut = lax.dynamic_slice_in_dim(query_cut, begin, count, 0)
    low = (own_sentence * CODES - 1).reshape(1, count)
    high_self = (own_sentence * CODES + own_cut).reshape(1, count)
    high_cross = (own_sentence * CODES + CODES // 2).reshape(1, count)
    first_row = first[DOC_LEN]
    last_row = jnp.sum(jnp.where(jnp.arange(sentence_lengths.shape[0]) <= own_sentence[-1], sentence_lengths, 0))
    origin = begin - DOC_LEN
    bounds = jnp.stack([(first_row - origin) // CHUNK, (last_row - origin + CHUNK - 1) // CHUNK]).astype(jnp.int32)

    def gathered(weight):
        return lax.all_gather(weight, "head", axis=0, tiled=True)

    def window_of(value):
        below = shifted(value[rows - DOC_LEN :], 1)
        above = shifted(value[:DOC_LEN], -1)
        whole = jnp.concatenate([below, value, above, jnp.zeros((spare, width), value.dtype)], axis=0)
        return lax.dynamic_slice_in_dim(whole, part * count, wide, 0)

    own = lax.dynamic_slice_in_dim(query_state, part * count, count, 0)
    own_out_grad = lax.dynamic_slice_in_dim(out_grad, part * count, count, 0)
    w_query_t, w_key_t, w_value_t = gathered(w_query.T), gathered(w_key.T), gathered(w_value.T)
    content_window = window_of(content)
    w_out_all = gathered(w_out)
    w_cross_query_t = gathered(w_cross_query.T)
    w_cross_key_t, w_cross_value_t = gathered(w_cross_key.T), gathered(w_cross_value.T)
    encoded_window = window_of(encoded)
    w_cross_out_all = gathered(w_cross_out)
    w_inner_all = lax.all_gather(w_inner, "head", axis=0)
    w_outer_all = lax.all_gather(w_outer, "head", axis=0)
    gain_self, gain_cross, gain_final = (g.reshape(1, width) for g in (gain_self, gain_cross, gain_final))

    stats = [((HEADS * PAIR, count), BF16), ((CHUNK, count), F32), ((HEADS, count), F32), ((HEADS, count), F32), ((width, count), BF16)]
    self_t, lse_self = call(
        self_kernel, [((width, count), F32), ((HEADS, count), F32)], stats, 1,
        bounds, own, content_window, code, low, high_self, w_query_t, w_key_t, w_value_t,
    )
    hidden_one, cross_t, lse_cross = call(
        cross_kernel, [((count, width), F32), ((width, count), F32), ((HEADS, count), F32)], stats, 1,
        bounds, own, self_t, w_out_all, gain_self, encoded_window, code, low, high_cross,
        w_cross_query_t, w_cross_key_t, w_cross_value_t,
    )
    hidden_units = w_inner.shape[1]
    mixed, resid_two_grad, w_cross_out_grad, w_inner_grad, w_outer_grad, gain_cross_grad, gain_final_grad = call(
        ffn_kernel,
        [
            ((count, width), BF16), ((count, width), F32), ((width, width), BF16), ((slices, width, hidden_units), BF16),
            ((slices, hidden_units, width), BF16), ((1, width), F32), ((1, width), F32),
        ],
        [
            ((count, width), F32), ((count, width), BF16), ((slices, count, hidden_units), F32),
            ((slices, count, hidden_units), BF16), ((count, width), F32),
        ], 0,
        hidden_one, cross_t, w_cross_out_all, gain_cross, w_inner_all, w_outer_all, gain_final, own_out_grad,
    )
    back = [
        ((HEADS * PAIR, count), BF16), ((HEADS * PAIR, count), BF16), ((PAIRS, 2 * count, PAIR), BF16),
        ((PAIRS, 2 * count, PAIR), BF16), ((HEADS, count), F32), ((CHUNK, count), F32), ((width, count), BF16),
        ((width, count), F32), ((width, width), F32), ((width, width), F32),
    ]
    square = ((width, width), BF16)
    resid_one_grad, encoded_part, w_cross_query_grad, w_cross_key_grad, w_cross_value_grad, w_out_grad, gain_self_grad = call(
        cross_back_kernel,
        [((count, width), F32), ((wide, width), BF16), square, square, square, square, ((1, width), F32)],
        back + [((count, width), F32), ((count, 1), F32)], 1,
        bounds, own, self_t, w_out_all, gain_self, resid_two_grad, w_cross_out_all, cross_t, lse_cross,
        encoded_window, code, low, high_cross, w_cross_query_t, w_cross_key_t, w_cross_value_t,
    )
    own_grad, content_part, w_query_grad, w_key_grad, w_value_grad = call(
        self_back_kernel, [((count, width), BF16), ((wide, width), BF16), square, square, square], back, 1,
        bounds, own, resid_one_grad, w_out_all, self_t, lse_self,
        content_window, code, low, high_self, w_query_t, w_key_t, w_value_t,
    )

    def returned(grad):
        place = jnp.zeros((2 * DOC_LEN + rows + spare, width), BF16)
        place = lax.dynamic_update_slice_in_dim(place, grad, part * count, 0)
        below = shifted(place[:DOC_LEN], -1).astype(F32)
        above = shifted(place[DOC_LEN + rows : 2 * DOC_LEN + rows], 1).astype(F32)
        whole = place[DOC_LEN : DOC_LEN + rows].astype(F32)
        whole = whole + jnp.pad(below, ((rows - DOC_LEN, 0), (0, 0))) + jnp.pad(above, ((0, rows - DOC_LEN), (0, 0)))
        return lax.psum(whole.astype(BF16), "head").astype(F32)

    def summed(grad):
        return lax.psum(lax.psum_scatter(grad, "head", scatter_dimension=0, tiled=True), "seq").astype(F32)

    def summed_t(grad):
        return summed(grad).T

    def summed_columns(grad):
        return lax.psum(lax.psum_scatter(grad, "head", scatter_dimension=1, tiled=True), "seq").astype(F32)

    def summed_gain(grad):
        return lax.psum(grad.reshape(width), ("seq", "head"))

    return (
        lax.all_gather(mixed, "head", axis=0, tiled=True),
        lax.all_gather(own_grad, "head", axis=0, tiled=True).astype(F32),
        returned(content_part),
        returned(encoded_part),
        summed_t(w_query_grad),
        summed_columns(w_key_grad),
        summed_columns(w_value_grad),
        summed(w_out_grad),
        summed_gain(gain_self_grad),
        summed_t(w_cross_query_grad),
        summed_columns(w_cross_key_grad),
        summed_columns(w_cross_value_grad),
        summed(w_cross_out_grad),
        summed_gain(gain_cross_grad),
        lax.psum(lax.psum_scatter(w_inner_grad, "head", scatter_dimension=0, tiled=False), "seq").astype(F32),
        lax.psum(lax.psum_scatter(w_outer_grad, "head", scatter_dimension=0, tiled=False), "seq").astype(F32),
        summed_gain(gain_final_grad),
    )


def solution(mesh):
    rows, whole, columns, split = P("seq", None), P(), P(None, "head"), P("head", None)
    in_specs = (
        rows, rows, rows, whole, whole, whole, columns, columns, columns, split, whole,
        columns, columns, columns, split, whole, columns, split, whole, rows,
    )
    out_specs = (
        rows, rows, rows, rows, columns, columns, columns, split, whole,
        columns, columns, columns, split, whole, columns, split, whole,
    )
    return jax.shard_map(body, mesh=mesh, in_specs=in_specs, out_specs=out_specs, check_vma=False)
```

time: 1300 us -> 918 us (0.71)
  matrix products: 277 us -> 0 us
  waiting for transfers between devices: 746 us -> 484 us
  blocking collectives: 30.1 us -> 193 us
  other arithmetic: 177 us -> 34.3 us
  Pallas kernels: 0 us -> 74 us
  starting transfers between devices: 10.9 us -> 61.7 us
    psum x7 -> x2, waiting for transfers between devices: 746 us -> 182 us  [the longest x1 120 us: returned(): return lax.psum(whole.astype(BF16), 'head').astype(F32)]
    dot_general x42 -> x0, matrix products: 277 us -> none  [the longest x2 65.2 us: attend_back(): jnp.einsum('qui,zui->uqz', gradient_cube, value_matrix.reshape(model_widt...]
    reduce_scatter x0 -> x6, waiting for transfers between devices: none -> 177 us  [the longest x4 87.2 us: summed(): lax.psum_scatter(grad, 'head', scatter_dimension=0, tiled=True)]
    all_gather x0 -> x8, blocking collectives: none -> 151 us  [gathered(): return lax.all_gather(weight, 'head', axis=0, tiled=True)]
    unnamed x7 -> x20, waiting for transfers between devices: 0.11 us -> 89.6 us
    pallas_call x0 -> x5, Pallas kernels: none -> 74 us  [call(): pl.pallas_call(kernel, out_shape=[jax.ShapeDtypeStruct(shape, kind) for s...]
    convert_element_type x14 -> x13, other arithmetic: 88 us -> 23.9 us  [the longest x4 9.18 us: returned(): return lax.psum(whole.astype(BF16), 'head').astype(F32)]
    reduce_sum x13 -> x2, other arithmetic: 65.4 us -> 1.78 us  [the longest x1 1.28 us: body(): jnp.sum(jnp.where(jnp.arange(sentence_lengths.shape[0]) <= own_sentence[-...]
  transfers between devices with their start and end apart: 11 -> 24, of which waited for: 7 -> 14; matrix products, arithmetic and copies ran while one was open for 5% -> 6% of each run, Pallas kernels for 0% -> 2%
where the time goes in v1:
time: 918 us; the launch traced here: 902 us
  waiting for transfers between devices  484 us (53%)
  blocking collectives  193 us (21%)
  Pallas kernels  74 us (8%)
  starting transfers between devices  61.7 us (7%)
  local copies, waits for them, and re-layouts  39 us (4%)
  other arithmetic  34.3 us (4%)
  between operations  15.8 us (2%)
    all_gather x8, blocking collectives, gathered(): return lax.all_gather(weight, 'head', axis=0, tiled=True)  151 us
    psum x1, waiting for transfers between devices, returned(): return lax.psum(whole.astype(BF16), 'head').astype(F32)  120 us
    unnamed x20, waiting for transfers between devices  89.6 us
    reduce_scatter x4, waiting for transfers between devices, summed(): lax.psum_scatter(grad, 'head', scatter_dimension=0, tiled=True)  87.2 us
    pallas_call x5, Pallas kernels, call(): pl.pallas_call(kernel, out_shape=[jax.ShapeDtypeStruct(shape, kind) for s...  74 us
    psum x1, waiting for transfers between devices, summed(): lax.psum(lax.psum_scatter(grad, 'head', scatter_dimension=0, tiled=True),...  62.7 us
    ppermute x8, starting transfers between devices, shifted(): lax.ppermute(value, 'seq', [(i, i + by) for i in range(peers) if 0 <= i +...  61.1 us
    reduce_scatter x1, waiting for transfers between devices, body(): lax.psum_scatter(w_outer_grad, 'head', scatter_dimension=0, tiled=False)  45.5 us
  transfers between devices with their start and end apart: 24, of which 14 were waited for; matrix products, arithmetic and copies ran while one was open for 6% of the time, Pallas kernels for 2%

profile of v1, /device:TPU:0, one launch (start us, length us, event | category | flops | bytes accessed | tf_op | source)
XLA Modules:
  0.0 901.6 jit_solution(4894098017361659211)
XLA Ops:
  12.4 4.0 collective-permute-start
  19.2 5.1 collective-permute-start.2
  43.5 23.4 %all_gather.48.w_value_t = bf16[512,512]{1,0:T(8,128)(2,1)} all-gather(bf16[128,512]{1,0:T(8,128)(2,1)} %bitcast.46), channel_id=1, replica_groups=mesh['seq'=8,'head'=4] {'head'}, dimensions={0}, use_global_device_ids=true | all-gather | bytes 655360 | tf_op jit(solution)/shard_map/all_gather | solution.py:339
  66.9 19.6 %all_gather.47.w_key_t = bf16[512,512]{1,0:T(8,128)(2,1)} all-gather(bf16[128,512]{1,0:T(8,128)(2,1)} %bitcast.45), channel_id=1, replica_groups=mesh['seq'=8,'head'=4] {'head'}, dimensions={0}, use_global_device_ids=true | all-gather | bytes 655360 | tf_op jit(solution)/shard_map/all_gather | solution.py:339
  86.5 21.6 %all_gather.46.w_query_t = bf16[512,512]{1,0:T(8,128)(2,1)} all-gather(bf16[128,512]{1,0:T(8,128)(2,1)S(1)} %bitcast.44), channel_id=1, replica_groups=mesh['seq'=8,'head'=4] {'head'}, dimensions={0}, use_global_device_ids=true | all-gather | bytes 655360 | tf_op jit(solution)/shard_map/all_gather | solution.py:339
  108.6 21.5 %all_gather.44.w_value_t = bf16[512,512]{1,0:T(8,128)(2,1)} all-gather(bf16[128,512]{1,0:T(8,128)(2,1)S(1)} %bitcast.43), channel_id=1, replica_groups=mesh['seq'=8,'head'=4] {'head'}, dimensions={0}, use_global_device_ids=true | all-gather | bytes 655360 | tf_op jit(solution)/shard_map/all_gather | solution.py:339
  130.2 16.7 %all_gather.43.w_key_t = bf16[512,512]{1,0:T(8,128)(2,1)} all-gather(bf16[128,512]{1,0:T(8,128)(2,1)S(1)} %bitcast.42), channel_id=1, replica_groups=mesh['seq'=8,'head'=4] {'head'}, dimensions={0}, use_global_device_ids=true | all-gather | bytes 655360 | tf_op jit(solution)/shard_map/all_gather | solution.py:339
  146.9 15.6 %all_gather.42.w_query_t = bf16[512,512]{1,0:T(8,128)(2,1)} all-gather(bf16[128,512]{1,0:T(8,128)(2,1)S(1)} %bitcast.41), channel_id=1, replica_groups=mesh['seq'=8,'head'=4] {'head'}, dimensions={0}, use_global_device_ids=true | all-gather | bytes 655360 | tf_op jit(solution)/shard_map/all_gather | solution.py:339
  162.5 16.9 %all_gather.45.w_out = bf16[512,512]{1,0:T(8,128)(2,1)} all-gather(bf16[128,512]{1,0:T(8,128)(2,1)S(1)} %copy-done.12), channel_id=1, replica_groups=mesh['seq'=8,'head'=4] {'head'}, dimensions={0}, use_global_device_ids=true | all-gather | bytes 655360 | tf_op jit(solution)/shard_map/all_gather | solution.py:339
  179.4 15.5 %all_gather.49.w_out.w_cross_out = bf16[512,512]{1,0:T(8,128)(2,1)} all-gather(bf16[128,512]{1,0:T(8,128)(2,1)S(1)} %copy-done.13), channel_id=1, replica_groups=mesh['seq'=8,'head'=4] {'head'}, dimensions={0}, use_global_device_ids=true | all-gather | bytes 655360 | tf_op jit(solution)/shard_map/all_gather | solution.py:339
  194.9 6.0 fusion.2
  200.9 9.4 %shard_map.323 = (f32[512,384]{1,0:T(8,128)}, f32[8,384]{1,0:T(8,128)}) custom-call(s32[2]{0:T(128)} %pad_add_fusion.bounds, bf16[384,512]{1,0:T(8,128)(2,1)} %constant_dynamic-slice_fusion.1.own, bf16[2560,512]{1,0:T(8,128)(2,1)} %get-tuple-element.162.window, s32[2560,1]{1,0:T(8,128)} %reshape.106.code, s32[1,384]{1,0:T(1,128)} %reshape.87.low, ...), custom_call_target="tpu_custom_call" | custom-call | tf_op jit(solution)/shard_map/pallas_call | solution.py:291
  210.3 10.8 %shard_map.324 = (f32[384,512]{1,0:T(8,128)}, f32[512,384]{1,0:T(8,128)}, f32[8,384]{1,0:T(8,128)}) custom-call(s32[2]{0:T(128)} %pad_add_fusion.bounds, bf16[384,512]{1,0:T(8,128)(2,1)} %constant_dynamic-slice_fusion.1.own, f32[512,384]{1,0:T(8,128)} %get-tuple-element.41.attn_t.self_t, bf16[512,512]{1,0:T(8,128)(2,1)} %all_gather.45.w_out, ...), custom_call_target="tpu_custom_call" | custom-call | tf_op jit(solution)/shard_map/pallas_call | solution.py:291
  221.1 12.6 %shard_map.325 = (bf16[384,512]{1,0:T(8,128)(2,1)}, f32[384,512]{1,0:T(8,128)}, bf16[512,512]{1,0:T(8,128)(2,1)}, bf16[4,512,512]{2,1,0:T(8,128)(2,1)}, bf16[4,5...) custom-call(f32[384,512]{1,0:T(8,128)} %get-tuple-element.42.hidden_one, ...), custom_call_target="tpu_custom_call" | custom-call | tf_op jit(solution)/shard_map/pallas_call | solution.py:291
  233.7 26.1 %shard_map.326 = (f32[384,512]{1,0:T(8,128)}, bf16[2560,512]{1,0:T(8,128)(2,1)}, bf16[512,512]{1,0:T(8,128)(2,1)}, bf16[512,512]{1,0:T(8,128)(2,1)}, bf16[512,51...) custom-call(s32[2]{0:T(128)} %pad_add_fusion.bounds, ...), custom_call_target="tpu_custom_call" | custom-call | tf_op jit(solution)/shard_map/pallas_call | solution.py:291
  259.8 15.2 %shard_map.327 = (bf16[384,512]{1,0:T(8,128)(2,1)}, bf16[2560,512]{1,0:T(8,128)(2,1)}, bf16[512,512]{1,0:T(8,128)(2,1)}, bf16[512,512]{1,0:T(8,128)(2,1)}, bf16[512,512]{1,0:T(8,128)(2,1)}) custom-call(s32[2]{0:T(128)} %pad_add_fusion.bounds, bf16[384,512]{1,0:T(8,128)(2,1)} %constant_dynamic-slice_fusion.1.own, ...), custom_call_target="tpu_custom_call" | custom-call | tf_op jit(solution)/shard_map/pallas_call | solution.py:291
  290.9 41.3 %collective-permute-start.5 = (bf16[1024,512]{1,0:T(8,128)(2,1)S(1)}, bf16[1024,512]{1,0:T(8,128)(2,1)S(1)}, u32[]{:S(2)}, u32[]{:S(2)}) collective-permute-start(bf16[1024,512]{1,0:T(8,128)(2,1)S(1)} %get-tuple-element.153), channel_id=1, source_target_pairs={{0,4},{4,8},{8,12},{12,16},{16,20},{20,24},{24,28},{1,5},{5,9},{9,... | collective-permute-start | bytes 3145736 | tf_op jit(solution)/shard_map/ppermute | solution.py:303
  334.3 5.1 collective-permute-start.7
  343.4 21.3 %reduce-scatter.31.cloned.1.call-done = bf16[128,512]{1,0:T(8,128)(2,1)} async-done(((bf16[512,512]{1,0:T(8,128)(2,1)}), bf16[128,512]{1,0:T(8,128)(2,1)}) %reduce-scatter.31.cloned.1.call-update) | async-done | bytes 131088
  366.3 21.0 %reduce-scatter.33.cloned.1.call-done = bf16[128,512]{1,0:T(8,128)(2,1)} async-done(((bf16[512,512]{1,0:T(8,128)(2,1)}), bf16[128,512]{1,0:T(8,128)(2,1)}) %reduce-scatter.33.cloned.1.call-update) | async-done | bytes 131088
  389.1 21.0 %reduce-scatter.35.cloned.1.call-done = bf16[128,512]{1,0:T(8,128)(2,1)} async-done(((bf16[512,512]{1,0:T(8,128)(2,1)}), bf16[128,512]{1,0:T(8,128)(2,1)}) %reduce-scatter.35.cloned.1.call-update) | async-done | bytes 131088
  411.7 20.4 %reduce-scatter.37.cloned.1.call-done = bf16[128,512]{1,0:T(8,128)(2,1)} async-done(((bf16[512,512]{1,0:T(8,128)(2,1)}), bf16[128,512]{1,0:T(8,128)(2,1)}) %reduce-scatter.37.cloned.1.call-update) | async-done | bytes 131088
  433.8 20.6 %reduce-scatter.19.cloned.1.call-done = bf16[128,512]{1,0:T(8,128)(2,1)} async-done(((bf16[512,512]{1,0:T(8,128)(2,1)}), bf16[128,512]{1,0:T(8,128)(2,1)}) %reduce-scatter.19.cloned.1.call-update) | async-done | bytes 131088 | tf_op jit(solution)/shard_map/reduce_scatter | solution.py:412
  454.4 22.2 %reduce-scatter.21.cloned.1.call-done = bf16[128,512]{1,0:T(8,128)(2,1)} async-done(((bf16[512,512]{1,0:T(8,128)(2,1)}), bf16[128,512]{1,0:T(8,128)(2,1)}) %reduce-scatter.21.cloned.1.call-update) | async-done | bytes 131088 | tf_op jit(solution)/shard_map/reduce_scatter | solution.py:412
  476.7 22.3 %reduce-scatter.23.cloned.1.call-done = bf16[128,512]{1,0:T(8,128)(2,1)} async-done(((bf16[512,512]{1,0:T(8,128)(2,1)}), bf16[128,512]{1,0:T(8,128)(2,1)}) %reduce-scatter.23.cloned.1.call-update) | async-done | bytes 131088 | tf_op jit(solution)/shard_map/reduce_scatter | solution.py:412
  498.9 22.1 %reduce-scatter.25.cloned.1.call-done = bf16[128,512]{1,0:T(8,128)(2,1)} async-done(((bf16[512,512]{1,0:T(8,128)(2,1)}), bf16[128,512]{1,0:T(8,128)(2,1)}) %reduce-scatter.25.cloned.1.call-update) | async-done | bytes 131088 | tf_op jit(solution)/shard_map/reduce_scatter | solution.py:412
  521.0 44.4 %reduce-scatter.27.cloned.1.call-done = bf16[1,512,512]{2,1,0:T(8,128)(2,1)} async-done(((bf16[4,512,512]{2,1,0:T(8,128)(2,1)}), bf16[1,512,512]{2,1,0:T(8,128)(2,1)}) %reduce-scatter.27.cloned.1.call-update) | async-done | bytes 524304 | tf_op jit(solution)/shard_map/reduce_scatter | solution.py:438
  565.5 45.5 %reduce-scatter.29.cloned.1.call-done = bf16[1,512,512]{2,1,0:T(8,128)(2,1)} async-done(((bf16[4,512,512]{2,1,0:T(8,128)(2,1)}), bf16[1,512,512]{2,1,0:T(8,128)(2,1)}) %reduce-scatter.29.cloned.1.call-update) | async-done | bytes 524304 | tf_op jit(solution)/shard_map/reduce_scatter | solution.py:439
  611.0 42.3 %all-reduce.6 = (f32[512]{0:T(512)}, f32[512]{0:T(512)}, f32[512]{0:T(512)}) all-reduce(f32[512]{0:T(512)S(1)} %bitcast.62, f32[512]{0:T(512)S(1)} %bitcast.60, f32[512]{0:T(512)S(1)} %bitcast.61), channel_id=1, replica_groups=mesh['seq'=8,'head'=4] {'seq','head'}, use_global_device_ids=true, to_apply=%region_15.16 | all-reduce | flops 1536 | bytes 12288 | tf_op jit(solution)/shard_map/psum | solution.py:421
  653.3 34.2 %all-gather.9.cloned.1.call-done = bf16[1536,512]{1,0:T(8,128)(2,1)} async-done(((bf16[384,512]{1,0:T(8,128)(2,1)}), bf16[1536,512]{1,0:T(8,128)(2,1)}) %all-gather.9.cloned.1.call-update) | async-done | bytes 1572880 | tf_op jit(solution)/shard_map/all_gather | solution.py:425
  690.9 119.7 %all-reduce.14.cloned.1.call-done = (bf16[1536,512]{1,0:T(8,128)(2,1)}, bf16[1536,512]{1,0:T(8,128)(2,1)}) async-done(((bf16[1536,512]{1,0:T(8,128)(2,1)}, bf16[1536,512]{1,0:T(8,128)(2,1)}), (bf16[1536,512]{1,0:T(8,128)(2,1)}, bf16[1536,512]{1,0:T(8,128)(2,1)})) %all-reduce.14.cloned.1.call-update) | async-done | bytes 3145744 | tf_op jit(solution)/shard_map/psum | solution.py:409
  816.3 62.7 %all-reduce.12.cloned.1.call-done = (bf16[512,128]{0,1:T(8,128)(2,1)}, bf16[512,128]{0,1:T(8,128)(2,1)}, bf16[512,128]{1,0:T(8,128)(2,1)}, bf16[512,128]{1,0:T(8...) async-done(((bf16[512,128]{0,1:T(8,128)(2,1)}, ...) | async-done | bytes 2097168 | tf_op jit(solution)/shard_map/psum | solution.py:412
  (151 shorter events, 79.8 us)
Async XLA Ops:
  7.2 213.9 %all-gather.11.cloned.1.call-start = ((), (), s32[]{:S(2)}) async-start(), calls=%async_computation.18 | async-start | bytes 2621440 | tf_op jit(solution)/shard_map/all_gather | solution.py:356
  7.9 213.1 %all-gather.13.cloned.1.call-start = ((), (), s32[]{:S(2)}) async-start(), calls=%async_computation.19 | async-start | bytes 2621440 | tf_op jit(solution)/shard_map/all_gather | solution.py:357
  11.0 183.9 %collective-permute-start.1 = (bf16[1024,512]{1,0:T(8,128)(2,1)}, bf16[1024,512]{1,0:T(8,128)(2,1)}, u32[]{:S(2)}, u32[]{:S(2)}) collective-permute-start(bf16[1024,512]{1,0:T(8,128)(2,1)} %get-tuple-element.156), channel_id=1, source_target_pairs={{4,0},{8,4},{12,8},{16,12},{20,16},{24,20},{28,24},{5,1},{9,5},{13... | collective-permute-start | bytes 3145736 | tf_op jit(solution)/shard_map/ppermute | solution.py:303
  12.4 182.4 %collective-permute-start = (bf16[1024,512]{1,0:T(8,128)(2,1)}, bf16[1024,512]{1,0:T(8,128)(2,1)}, u32[]{:S(2)}, u32[]{:S(2)}) collective-permute-start(bf16[1024,512]{1,0:T(8,128)(2,1)} %get-tuple-element.157), channel_id=1, source_target_pairs={{0,4},{4,8},{8,12},{12,16},{16,20},{20,24},{24,28},{1,5},{5,9},{9,... | collective-permute-start | bytes 3145736 | tf_op jit(solution)/shard_map/ppermute | solution.py:303
  17.9 176.9 %collective-permute-start.3 = (bf16[1024,512]{1,0:T(8,128)(2,1)}, bf16[1024,512]{1,0:T(8,128)(2,1)}, u32[]{:S(2)}, u32[]{:S(2)}) collective-permute-start(bf16[1024,512]{1,0:T(8,128)(2,1)} %get-tuple-element.154), channel_id=1, source_target_pairs={{4,0},{8,4},{12,8},{16,12},{20,16},{24,20},{28,24},{5,1},{9,5},{13... | collective-permute-start | bytes 3145736 | tf_op jit(solution)/shard_map/ppermute | solution.py:303
  19.2 175.7 %collective-permute-start.2 = (bf16[1024,512]{1,0:T(8,128)(2,1)}, bf16[1024,512]{1,0:T(8,128)(2,1)}, u32[]{:S(2)}, u32[]{:S(2)}) collective-permute-start(bf16[1024,512]{1,0:T(8,128)(2,1)} %get-tuple-element.155), channel_id=1, source_target_pairs={{0,4},{4,8},{8,12},{12,16},{16,20},{20,24},{24,28},{1,5},{5,9},{9,... | collective-permute-start | bytes 3145736 | tf_op jit(solution)/shard_map/ppermute | solution.py:303
  24.3 340.4 %reduce-scatter.31.cloned.1.call-start = ((), (), s32[]{:S(2)}) async-start(), calls=%async_computation.20 | async-start | bytes 655360
  40.8 45.7 %copy-start.9 = (bf16[512,128]{0,1:T(8,128)(2,1)S(1)}, bf16[512,128]{0,1:T(8,128)(2,1)}, u32[]{:S(2)}) copy-start(bf16[512,128]{0,1:T(8,128)(2,1)} %copy.73) | copy-start | bytes 393220
  40.9 121.6 %copy-start.12 = (bf16[128,512]{1,0:T(8,128)(2,1)S(1)}, bf16[128,512]{1,0:T(8,128)(2,1)}, u32[]{:S(2)}) copy-start(bf16[128,512]{1,0:T(8,128)(2,1)} %param.29) | copy-start | bytes 393220
  41.7 137.7 %copy-start.13 = (bf16[128,512]{1,0:T(8,128)(2,1)S(1)}, bf16[128,512]{1,0:T(8,128)(2,1)}, u32[]{:S(2)}) copy-start(bf16[128,512]{1,0:T(8,128)(2,1)} %param.34) | copy-start | bytes 393220
  43.5 151.4 %copy-start.3 = (bf16[1536,512]{1,0:T(8,128)(2,1)S(1)}, bf16[1536,512]{1,0:T(8,128)(2,1)}, u32[]{:S(2)}) copy-start(bf16[1536,512]{1,0:T(8,128)(2,1)} %param.21) | copy-start | bytes 4718596
  277.1 110.3 %reduce-scatter.33.cloned.1.call-start = ((), (), s32[]{:S(2)}) async-start(), calls=%async_computation.21 | async-start | bytes 655360
  279.2 130.8 %reduce-scatter.35.cloned.1.call-start = ((), (), s32[]{:S(2)}) async-start(), calls=%async_computation.22 | async-start | bytes 655360
  280.3 151.9 %reduce-scatter.37.cloned.1.call-start = ((), (), s32[]{:S(2)}) async-start(), calls=%async_computation.23 | async-start | bytes 655360
  281.4 173.0 %reduce-scatter.19.cloned.1.call-start = ((), (), s32[]{:S(2)}) async-start(), calls=%async_computation.12 | async-start | bytes 655360 | tf_op jit(solution)/shard_map/reduce_scatter | solution.py:412
  282.2 194.5 %reduce-scatter.21.cloned.1.call-start = ((), (), s32[]{:S(2)}) async-start(), calls=%async_computation.13 | async-start | bytes 655360 | tf_op jit(solution)/shard_map/reduce_scatter | solution.py:412
  282.9 216.0 %reduce-scatter.23.cloned.1.call-start = ((), (), s32[]{:S(2)}) async-start(), calls=%async_computation.14 | async-start | bytes 655360 | tf_op jit(solution)/shard_map/reduce_scatter | solution.py:412
  283.6 237.4 %reduce-scatter.25.cloned.1.call-start = ((), (), s32[]{:S(2)}) async-start(), calls=%async_computation.15 | async-start | bytes 655360 | tf_op jit(solution)/shard_map/reduce_scatter | solution.py:412
  284.2 281.2 %reduce-scatter.27.cloned.1.call-start = ((), (), s32[]{:S(2)}) async-start(), calls=%async_computation.16 | async-start | bytes 2621440 | tf_op jit(solution)/shard_map/reduce_scatter | solution.py:438
  285.0 326.0 %reduce-scatter.29.cloned.1.call-start = ((), (), s32[]{:S(2)}) async-start(), calls=%async_computation.17 | async-start | bytes 2621440 | tf_op jit(solution)/shard_map/reduce_scatter | solution.py:439
  285.5 367.7 %all-gather.7.cloned.1.call-start = ((), (), s32[]{:S(2)}) async-start(), calls=%async_computation.10 | async-start | bytes 1966080 | tf_op jit(solution)/shard_map/all_gather | solution.py:424
  286.3 401.1 %all-gather.9.cloned.1.call-start = ((), (), s32[]{:S(2)}) async-start(), calls=%async_computation.11 | async-start | bytes 1966080 | tf_op jit(solution)/shard_map/all_gather | solution.py:425
  286.9 523.7 %all-reduce.14.cloned.1.call-start = ((), (), s32[]{:S(2)}) async-start(), calls=%async_computation.25 | async-start | bytes 6291456 | tf_op jit(solution)/shard_map/psum | solution.py:409
  289.3 43.2 %copy-start.4 = (bf16[2560,512]{1,0:T(8,128)(2,1)S(1)}, bf16[2560,512]{1,0:T(8,128)(2,1)}, u32[]{:S(2)}) copy-start(bf16[2560,512]{1,0:T(8,128)(2,1)} %get-tuple-element.51) | copy-start | bytes 7864324
  289.4 50.0 %collective-permute-start.4 = (bf16[1024,512]{1,0:T(8,128)(2,1)S(1)}, bf16[1024,512]{1,0:T(8,128)(2,1)S(1)}, u32[]{:S(2)}, u32[]{:S(2)}) collective-permute-start(bf16[1024,512]{1,0:T(8,128)(2,1)S(1)} %get-tuple-element.152), channel_id=1, source_target_pairs={{4,0},{8,4},{12,8},{16,12},{20,16},{24,20},{28,24},{5,1},{9,5},{13... | collective-permute-start | bytes 3145736 | tf_op jit(solution)/shard_map/ppermute | solution.py:303
  290.9 48.5 %collective-permute-start.5 = (bf16[1024,512]{1,0:T(8,128)(2,1)S(1)}, bf16[1024,512]{1,0:T(8,128)(2,1)S(1)}, u32[]{:S(2)}, u32[]{:S(2)}) collective-permute-start(bf16[1024,512]{1,0:T(8,128)(2,1)S(1)} %get-tuple-element.153), channel_id=1, source_target_pairs={{0,4},{4,8},{8,12},{12,16},{16,20},{20,24},{24,28},{1,5},{5,9},{9,... | collective-permute-start | bytes 3145736 | tf_op jit(solution)/shard_map/ppermute | solution.py:303
  333.0 8.1 collective-permute-start.6
  334.3 7.3 collective-permute-start.7
  343.3 267.7 %copy-start.19 = (f32[1,512]{1,0:T(1,128)S(1)}, f32[1,512]{1,0:T(1,128)}, u32[]{:S(2)}) copy-start(f32[1,512]{1,0:T(1,128)} %get-tuple-element.61) | copy-start | bytes 6148
  343.3 267.7 %copy-start.20 = (f32[1,512]{1,0:T(1,128)S(1)}, f32[1,512]{1,0:T(1,128)}, u32[]{:S(2)}) copy-start(f32[1,512]{1,0:T(1,128)} %get-tuple-element.64) | copy-start | bytes 6148
  343.3 267.7 %copy-start.21 = (f32[1,512]{1,0:T(1,128)S(1)}, f32[1,512]{1,0:T(1,128)}, u32[]{:S(2)}) copy-start(f32[1,512]{1,0:T(1,128)} %get-tuple-element.56) | copy-start | bytes 6148
  343.3 535.7 %all-reduce.12.cloned.1.call-start = ((), (), s32[]{:S(2)}) async-start(), calls=%async_computation.24 | async-start | bytes 4194304 | tf_op jit(solution)/shard_map/psum | solution.py:412
  (14 other events, 167.8 us)
Sparse Core Ops, SparseCore 0:
  9.6 56.3 all-gather.10
  67.6 64.7 all-gather.12
  277.2 87.4 reduce-scatter.30
  367.4 19.9 reduce-scatter.32
  390.1 19.9 reduce-scatter.34
  412.2 19.9 reduce-scatter.36
  434.4 19.9 reduce-scatter.18
  456.7 19.9 reduce-scatter.20
  478.9 19.9 reduce-scatter.22
  501.0 19.9 reduce-scatter.24
  523.3 42.1 reduce-scatter.26
  567.7 43.1 reduce-scatter.28
  612.5 37.4 all-gather.6
  651.4 35.9 all-gather.8
  690.3 120.2 all-reduce.13
  815.4 63.6 all-reduce.11

commit v2 on v1

--- a/solution.py
+++ b/solution.py
@@ -71,6 +71,529 @@
     zero = jnp.zeros_like(both)
     target[p, 0:rows, :] = jnp.where(lane < HEAD_SIZE, both, zero)
     target[p, rows : 2 * rows, :] = jnp.where(lane < HEAD_SIZE, zero, both)
+
+
+MESH = pl.DeviceIdType.MESH
+
+
+class Copies:
+    def __init__(self, send, recv, local):
+        self.send, self.recv, self.local = send, recv, local
+        self.remotes, self.locals = 0, 0
+
+    def remote(self, source, target, seq, part):
+        k = self.remotes
+        self.remotes += 1
+        return pltpu.make_async_remote_copy(
+            src_ref=source, dst_ref=target, send_sem=self.send.at[k], recv_sem=self.recv.at[k],
+            device_id=(seq, part), device_id_type=MESH,
+        )
+
+    def own(self, source, target):
+        k = self.locals
+        self.locals += 1
+        return pltpu.make_async_copy(source, target, self.local.at[k])
+
+
+def greet(seq, part, peers, slices):
+    barrier = pltpu.get_barrier_semaphore()
+    for d in range(1, peers):
+        pl.semaphore_signal(barrier, inc=1, device_id=(lax.rem(seq + d, peers), part), device_id_type=MESH)
+    for d in range(1, slices):
+        pl.semaphore_signal(barrier, inc=1, device_id=(seq, lax.rem(part + d, slices)), device_id_type=MESH)
+    pl.semaphore_wait(barrier, peers - 1 + slices - 1)
+
+
+def halo_sizes(part, count, rows):
+    return max(0, DOC_LEN - part * count), max(0, (part + 1) * count + DOC_LEN - rows)
+
+
+def start_kernel(
+    peers, slices, count, content, encoded, pack_one, pack_two, pack_three,
+    content_window, encoded_window, all_one, all_two, all_three, send, recv, local, zeros,
+):
+    seq, part = lax.axis_index("seq"), lax.axis_index("head")
+    chip, core = seq // 2, lax.rem(seq, 2)
+    chips = peers // 2
+    sibling = chip * 2 + 1 - core
+    rows = content.shape[0]
+    span = count + 2 * DOC_LEN
+    spare = content_window.shape[0] - span
+    copies = Copies(send, recv, local)
+    zeros[...] = jnp.zeros_like(zeros)
+    greet(seq, part, peers, slices)
+    waits = []
+
+    def halo(source, window):
+        for k in range(slices):
+            below, above = halo_sizes(k, count, rows)
+            low = max(0, k * count - DOC_LEN)
+            inner = span - below - above
+            mine = copies.own(source.at[pl.ds(low, inner)], window.at[pl.ds(below, inner)])
+            tail = copies.own(zeros.at[pl.ds(0, spare)], window.at[pl.ds(span, spare)])
+            up = down = fill_low = fill_high = None
+            if below:
+                up = copies.remote(source.at[pl.ds(rows - below, below)], window.at[pl.ds(0, below)], seq + 1, part)
+                fill_low = copies.own(zeros.at[pl.ds(0, below)], window.at[pl.ds(0, below)])
+            if above:
+                down = copies.remote(source.at[pl.ds(0, above)], window.at[pl.ds(span - above, above)], seq - 1, part)
+                fill_high = copies.own(zeros.at[pl.ds(0, above)], window.at[pl.ds(span - above, above)])
+            here, first, last = part == k, seq == 0, seq == peers - 1
+
+            def start(mine=mine, tail=tail, up=up, down=down, fill_low=fill_low, fill_high=fill_high, here=here):
+                @pl.when(here)
+                def _():
+                    if up is not None:
+                        pl.when(jnp.logical_not(last))(up.start)
+                        pl.when(first)(fill_low.start)
+                    if down is not None:
+                        pl.when(jnp.logical_not(first))(down.start)
+                        pl.when(last)(fill_high.start)
+                    mine.start()
+                    tail.start()
+
+            def finish(mine=mine, tail=tail, up=up, down=down, fill_low=fill_low, fill_high=fill_high, here=here):
+                @pl.when(here)
+                def _():
+                    if up is not None:
+                        pl.when(jnp.logical_not(last))(up.wait_send)
+                        pl.when(jnp.logical_not(first))(up.wait_recv)
+                        pl.when(first)(fill_low.wait)
+                    if down is not None:
+                        pl.when(jnp.logical_not(first))(down.wait_send)
+                        pl.when(jnp.logical_not(last))(down.wait_recv)
+                        pl.when(last)(fill_high.wait)
+                    mine.wait()
+                    tail.wait()
+
+            start()
+            waits.append(finish)
+
+    packs = ((pack_one, all_one), (pack_two, all_two), (pack_three, all_three))
+
+    def piece(ref, owner, index, size):
+        return ref.at[owner, pl.ds(pl.multiple_of(index * size, 16), size)]
+
+    across = {}
+    for n, (pack, whole) in enumerate(packs):
+        size = pack.shape[0] // peers
+        for d in range(1, slices):
+            to = lax.rem(part + d, slices)
+            source = pack.at[pl.ds(pl.multiple_of(seq * size, 16), size)]
+            across[n, d] = copies.remote(source, piece(whole, part, seq, size), seq, to)
+            across[n, d].start()
+        mine = copies.own(pack, whole.at[part])
+        mine.start()
+        waits.append(mine.wait)
+        if n == 0:
+            halo(content, content_window)
+    round_plane, to_sibling = {}, {}
+    for n, (pack, whole) in enumerate(packs):
+        size = pack.shape[0] // peers
+        for d in range(1, slices):
+            across[n, d].wait_recv()
+            owner = lax.rem(part + slices - d, slices)
+            got = piece(whole, owner, seq, size)
+            for e in range(1, chips):
+                round_plane[n, d, e] = copies.remote(got, got, lax.rem(chip + e, chips) * 2 + core, part)
+                round_plane[n, d, e].start()
+            to_sibling[n, d, 0] = copies.remote(got, got, sibling, part)
+            to_sibling[n, d, 0].start()
+    halo(encoded, encoded_window)
+    for n, (pack, whole) in enumerate(packs):
+        size = pack.shape[0] // peers
+        for d in range(1, slices):
+            owner = lax.rem(part + slices - d, slices)
+            for e in range(1, chips):
+                round_plane[n, d, e].wait_recv()
+                got = piece(whole, owner, lax.rem(chip + chips - e, chips) * 2 + core, size)
+                to_sibling[n, d, e] = copies.remote(got, got, sibling, part)
+                to_sibling[n, d, e].start()
+    for copy in to_sibling.values():
+        copy.wait_recv()
+    for copy in (*across.values(), *round_plane.values(), *to_sibling.values()):
+        copy.wait_send()
+    for wait in waits:
+        wait()
+
+
+def add_rows(target, source, target_at, source_at, size):
+    step = 64 if size % 64 == 0 else 16
+
+    def one(i, carry):
+        to = pl.ds(pl.multiple_of(target_at + i * step, 16), step)
+        by = pl.ds(pl.multiple_of(source_at + i * step, 16), step)
+        target[to, :] = (target[to, :].astype(F32) + source[by, :].astype(F32)).astype(BF16)
+        return carry
+
+    lax.fori_loop(0, size // step, one, 0)
+
+
+def end_kernel(
+    peers, slices, count, blocks, parts, packs, plane_sums, outs, part_outs, pack_outs, scratch,
+):
+    seq, part = lax.axis_index("seq"), lax.axis_index("head")
+    chip, core = seq // 2, lax.rem(seq, 2)
+    chips = peers // 2
+    sibling = chip * 2 + 1 - core
+    rows = slices * count
+    span = count + 2 * DOC_LEN
+    send, recv, local = scratch[:3]
+    copies = Copies(send, recv, local)
+    first, last = seq == 0, seq == peers - 1
+    start_line, end_line = part == 0, part == slices - 1
+    greet(seq, part, peers, slices)
+    sent = []
+
+    def block(ref, index):
+        return ref.at[pl.ds(pl.multiple_of(index * count, 16), count)]
+
+    weight_scratch = scratch[3 : 3 + 5 * len(packs)]
+    to_core, held = [], []
+    for n, pack in enumerate(packs):
+        half = pack.shape[1] // 2
+        sibling_sum, mine = weight_scratch[5 * n : 5 * n + 2]
+        copy = copies.remote(pack.at[:, pl.ds(pl.multiple_of((1 - core) * half, 16), half)], sibling_sum, sibling, part)
+        copy.start()
+        to_core.append(copy)
+        keep = copies.own(pack.at[:, pl.ds(pl.multiple_of(core * half, 16), half)], mine)
+        keep.start()
+        held.append(keep)
+        sent.append(copy)
+
+    part_scratch = scratch[3 + 5 * len(packs) :]
+    halos = []
+    for n, grad in enumerate(parts):
+        total, from_above, from_below = part_scratch[5 * n : 5 * n + 3]
+        for k in range(slices):
+            below, above = halo_sizes(k, count, rows)
+            low = max(0, k * count - DOC_LEN)
+            inner = span - below - above
+            mine = copies.own(grad.at[pl.ds(below, inner)], total.at[pl.ds(low, inner)])
+            down = up = None
+            if below:
+                down = copies.remote(grad.at[pl.ds(0, below)], from_above.at[pl.ds(0, below)], seq - 1, part)
+            if above:
+                up = copies.remote(grad.at[pl.ds(span - above, above)], from_below.at[pl.ds(0, above)], seq + 1, part)
+            halos.append((n, k, below, above, low, inner, mine, down, up))
+
+            @pl.when(part == k)
+            def _(low=low, inner=inner, mine=mine, down=down, up=up, total=total):
+                if down is not None:
+                    pl.when(jnp.logical_not(first))(down.start)
+                if up is not None:
+                    pl.when(jnp.logical_not(last))(up.start)
+                mine.start()
+                if low:
+                    total[0:low, :] = jnp.zeros((low, total.shape[1]), BF16)
+                if low + inner < rows:
+                    total[low + inner : rows, :] = jnp.zeros((rows - low - inner, total.shape[1]), BF16)
+
+    def finish_halo(which):
+        for n, k, below, above, low, inner, mine, down, up in halos:
+            if n != which:
+                continue
+            total, from_above, from_below = part_scratch[5 * n : 5 * n + 3]
+
+            @pl.when(part == k)
+            def _(below=below, above=above, mine=mine, down=down, up=up, total=total, from_above=from_above, from_below=from_below):
+                mine.wait()
+                if down is not None:
+                    pl.when(jnp.logical_not(first))(down.wait_send)
+
+                    @pl.when(jnp.logical_not(last))
+                    def _():
+                        down.wait_recv()
+                        add_rows(total, from_above, rows - below, 0, below)
+
+                if up is not None:
+                    pl.when(jnp.logical_not(last))(up.wait_send)
+
+                    @pl.when(jnp.logical_not(first))
+                    def _():
+                        up.wait_recv()
+                        add_rows(total, from_below, 0, 0, above)
+
+    halves = 2 if slices <= 4 else 1
+    sub = count // halves
+
+    def unit_rows(ref, index, h):
+        return ref.at[pl.ds(index * count + h * sub, sub)]
+
+    def gather_rounds(out, me):
+        rounds, flows = {}, ((1, slices - 1 - me), (-1, me))
+        for sign, onward in flows:
+            behind = me if sign > 0 else slices - 1 - me
+            sends, waits = {}, {}
+            for k in range(behind + 1):
+                for h in range(halves):
+                    ref = unit_rows(out, me - sign * k, h)
+                    if onward:
+                        sends[k * halves + h] = ref
+                    if k:
+                        waits[k * halves + h] = ref
+            rounds[sign] = (sends, waits)
+        return rounds
+
+    def line_gather(out, me, sems):
+        steps, ends = [], []
+        ring = gather_rounds(out, me)
+        copies_of = {}
+        for sign in (1, -1):
+            sends, waits = ring[sign]
+            for i, ref in sends.items():
+                copies_of[sign, i] = sems(sign, i, ref, ref, me + sign)
+
+        def step(i):
+            for sign in (1, -1):
+                sends, waits = ring[sign]
+                if i in waits:
+                    sems(sign, i - halves, waits[i], waits[i], me).wait_recv()
+                if i in sends:
+                    if i:
+                        copies_of[sign, i - 1].wait_send()
+                    copies_of[sign, i].start()
+
+        def finish():
+            for sign in (1, -1):
+                sends, _ = ring[sign]
+                if sends:
+                    copies_of[sign, max(sends)].wait_send()
+
+        return [partial(step, i) for i in range(slices * halves)], finish
+
+    def line_sum(total, ins, out, me, sems):
+        units = (slices - 1) * halves
+        copies_of, before = {}, {1: None, -1: None}
+
+        def place(sign, i):
+            b = slices - 1 - i // halves if sign > 0 else i // halves
+            return b, unit_rows(total, b, i % halves)
+
+        def step(r):
+            for sign in (1, -1):
+                depth = me if sign > 0 else slices - 1 - me
+                i = r - depth
+                if not 0 <= i < units:
+                    continue
+                b, ref = place(sign, i)
+                passes = b > me if sign > 0 else b < me
+                slot = ins[0 if sign > 0 else 1].at[i]
+                if (passes or b == me) and depth:
+                    sems(sign, i, slot, slot, me).wait_recv()
+                    add_rows(total, slot, b * count + (i % halves) * sub, 0, sub)
+                if passes:
+                    if before[sign] is not None:
+                        before[sign].wait_send()
+                    before[sign] = sems(sign, i, ref, slot, me + sign)
+                    before[sign].start()
+
+        def finish():
+            for sign in (1, -1):
+                if before[sign] is not None:
+                    before[sign].wait_send()
+
+        def place_own():
+            out[pl.ds(me * count, count), :] = total[pl.ds(me * count, count), :]
+
+        return [partial(step, r) for r in range(units + slices - 1)], place_own, finish
+
+    def semaphores(units):
+        base = copies.remotes
+        copies.remotes += 2 * units
+
+        def make(sign, i, source, target, to):
+            k = base + i + (0 if sign > 0 else units)
+            return pltpu.make_async_remote_copy(
+                src_ref=source, dst_ref=target, send_sem=send.at[k], recv_sem=recv.at[k],
+                device_id=(seq, to), device_id_type=MESH,
+            )
+
+        return make
+
+    def interleave(*lists):
+        for k in range(max((len(steps) for steps in lists), default=0)):
+            for steps in lists:
+                if k < len(steps):
+                    steps[k]()
+
+    def at_place(run):
+        for me in range(slices):
+            pl.when(part == me)(partial(run, me))
+
+    own_copies = []
+    for own, out in zip(blocks, outs):
+        mine = copies.own(own, block(out, part))
+        mine.start()
+        own_copies.append(mine)
+    block_sems = [semaphores(slices * halves) for _ in outs]
+    sum_sems = [semaphores(slices * halves) for _ in part_outs]
+    after_sems = [semaphores(slices * halves) for _ in part_outs]
+
+    to_chips = []
+    for n, pack in enumerate(packs):
+        half = pack.shape[1] // 2
+        size = half // chips
+        sibling_sum, mine, by_chip = weight_scratch[5 * n : 5 * n + 3]
+        held[n].wait()
+        to_core[n].wait_recv()
+
+        def add_half(z, carry, sibling_sum=sibling_sum, mine=mine, half=half):
+            add_rows(mine.at[z], sibling_sum.at[z], 0, 0, half)
+            return carry
+
+        lax.fori_loop(0, slices, add_half, 0)
+        for e in range(1, chips):
+            to = lax.rem(chip + e, chips)
+            copy = copies.remote(mine.at[:, pl.ds(pl.multiple_of(to * size, 16), size)], by_chip.at[e - 1], to * 2 + core, part)
+            copy.start()
+            to_chips.append((n, e, copy))
+            sent.append(copy)
+    for mine in own_copies:
+        mine.wait()
+    for n in range(len(parts)):
+        finish_halo(n)
+
+    def first_section(me):
+        lists, ends = [], []
+        for out, sems in zip(outs, block_sems):
+            steps, finish = line_gather(out, me, sems)
+            lists.append(steps)
+            ends.append(finish)
+        for n, out in enumerate(part_outs):
+            total, _, _, right_in, left_in = part_scratch[5 * n : 5 * n + 5]
+            steps, place_own, finish = line_sum(total, (right_in, left_in), out, me, sum_sems[n])
+            lists.append(steps)
+            ends += [finish, place_own]
+        interleave(*lists)
+        for finish in ends:
+            finish()
+
+    at_place(first_section)
+
+    to_slices = []
+
+    def share(n, plane_sum, by_slice):
+        for d in range(1, slices):
+            to = lax.rem(part + d, slices)
+            copy = copies.remote(plane_sum.at[to], by_slice.at[d - 1], seq, to)
+            copy.start()
+            to_slices.append((n, copy))
+            sent.append(copy)
+
+    for n, pack in enumerate(packs):
+        half = pack.shape[1] // 2
+        size = half // chips
+        mine, by_chip, plane_sum, by_slice = weight_scratch[5 * n + 1 : 5 * n + 5]
+        for m, e, copy in to_chips:
+            if m == n:
+                copy.wait_recv()
+
+        def add_plane(i, carry, mine=mine, by_chip=by_chip, plane_sum=plane_sum, size=size):
+            z, r = i // (size // 16), lax.rem(i, size // 16)
+            at = pl.ds(pl.multiple_of(r * 16, 16), 16)
+            value = mine[z, pl.ds(pl.multiple_of(chip * size + r * 16, 16), 16), :].astype(F32)
+            for e in range(chips - 1):
+                value = value + by_chip[e, z, at, :].astype(F32)
+            plane_sum[z, at, :] = value.astype(BF16)
+            return carry
+
+        lax.fori_loop(0, slices * (size // 16), add_plane, 0)
+        share(n, plane_sum, by_slice)
+    plane_scratch = part_scratch[5 * len(parts) :]
+    for n, summed in enumerate(plane_sums):
+        plane_sum, by_slice = plane_scratch[2 * n : 2 * n + 2]
+        keep = copies.own(summed, plane_sum)
+        keep.start()
+        keep.wait()
+        share(len(packs) + n, plane_sum, by_slice)
+
+    def piece_at(n, of_chip, of_core):
+        size = pack_outs[n].shape[0] // peers
+        index = of_core * chips + of_chip if n < len(packs) else of_chip * 2 + of_core
+        return pl.multiple_of(index * size, 16), size
+
+    round_plane, to_sibling = [], []
+
+    def back_to_plane():
+        for n, out in enumerate(pack_outs):
+            if n < len(packs):
+                plane_sum, by_slice = weight_scratch[5 * n + 3 : 5 * n + 5]
+            else:
+                plane_sum, by_slice = plane_scratch[2 * (n - len(packs)) : 2 * (n - len(packs)) + 2]
+            start, size = piece_at(n, chip, core)
+            for m, copy in to_slices:
+                if m == n:
+                    copy.wait_recv()
+
+            def add_slices(r, carry, plane_sum=plane_sum, by_slice=by_slice, out=out, start=start):
+                at = pl.ds(pl.multiple_of(r * 16, 16), 16)
+                value = plane_sum[part, at, :].astype(F32)
+                for d in range(slices - 1):
+                    value = value + by_slice[d, at, :].astype(F32)
+                out[pl.ds(pl.multiple_of(start + r * 16, 16), 16), :] = value.astype(BF16)
+                return carry
+
+            lax.fori_loop(0, size // 16, add_slices, 0)
+            piece = out.at[pl.ds(start, size)]
+            for e in range(1, chips):
+                copy = copies.remote(piece, piece, lax.rem(chip + e, chips) * 2 + core, part)
+                copy.start()
+                round_plane.append((n, e, copy))
+                sent.append(copy)
+            copy = copies.remote(piece, piece, sibling, part)
+            copy.start()
+            round_plane.append((n, 0, copy))
+            sent.append(copy)
+
+    def second_section(me, low, high):
+        lists, ends = [], []
+        for out, sems in zip(part_outs, after_sems):
+            steps, finish = line_gather(out, me, sems)
+            lists.append(steps[low:high])
+            if high >= len(steps):
+                ends.append(finish)
+        interleave(*lists)
+        for finish in ends:
+            finish()
+
+    middle = slices * halves // 2 + 1
+    at_place(lambda me: second_section(me, 0, middle))
+    back_to_plane()
+    at_place(lambda me: second_section(me, middle, slices * halves))
+    for n, e, copy in round_plane:
+        copy.wait_recv()
+        if e:
+            start, size = piece_at(n, lax.rem(chip + chips - e, chips), core)
+            piece = pack_outs[n].at[pl.ds(start, size)]
+            copy = copies.remote(piece, piece, sibling, part)
+            copy.start()
+            to_sibling.append(copy)
+            sent.append(copy)
+    for copy in to_sibling:
+        copy.wait_recv()
+    for copy in sent:
+        copy.wait_send()
+
+
+class Rows:
+    def __init__(self, pack, index, size):
+        self.pack, self.at = pack, slice(index * size, (index + 1) * size)
+
+    def __getitem__(self, _):
+        value = self.pack[:, self.at, :]
+        return value.reshape(value.shape[0] * value.shape[1], value.shape[2])
+
+
+def write_rows(pack, index, size, value):
+    slices = pack.shape[0]
+    pack[:, index * size : (index + 1) * size, :] = value.astype(BF16).reshape(slices, size, value.shape[1])
+
+
+def write_pieces(pack, z, row, value):
+    size = pack.shape[2]
+    for i in range(value.shape[0] // size):
+        pack[row // size + i, z] = value[i * size : (i + 1) * size, :].astype(BF16)
 
 
 def mask_bias(code, low, high):
@@ -162,7 +685,8 @@
     lax.fori_loop(bounds[0], bounds[1], step, 0)
 
 
-def self_kernel(bounds, own, window, code, low, high, w_query_t, w_key_t, w_value_t, out, lse, spread, bias, top, total, low_t):
+def self_kernel(cols, bounds, own, window, code, low, high, pack_one, out, lse, spread, bias, top, total, low_t):
+    w_query_t, w_key_t, w_value_t = (Rows(pack_one, k, cols) for k in range(3))
     low_t[...] = dot_nt(w_query_t[...], own[...]).astype(BF16)
     spread_heads(low_t, spread)
     attend(bounds, window, code, low, high, w_key_t, w_value_t, spread, bias, top, total, out)
@@ -170,9 +694,9 @@
 
 
 def cross_kernel(
-    bounds, own, attn_t, w_out, gain, window, code, low, high, w_query_t, w_key_t, w_value_t,
-    hidden, out, lse, spread, bias, top, total, low_t,
+    cols, bounds, own, attn_t, gain, window, code, low, high, pack_two, hidden, out, lse, spread, bias, top, total, low_t,
 ):
+    w_out, w_query_t, w_key_t, w_value_t = (Rows(pack_two, k, cols) for k in range(4))
     branch = dot_tn(attn_t[...].astype(BF16), w_out[...])
     normed, _ = layer_norm(own[...].astype(F32) + branch)
     hidden[...] = normed * gain[...]
@@ -183,11 +707,12 @@
 
 
 def ffn_kernel(
-    hidden_one, cross_t, w_out, gain_cross, w_inner, w_outer, gain_final, out_grad,
-    mixed, resid_grad, w_out_grad, w_inner_grad, w_outer_grad, gain_cross_grad, gain_final_grad,
+    cols, hidden_one, cross_t, pack_two, gain_cross, pack_three, gain_final, out_grad,
+    mixed, resid_grad, w_out_grad, grad_three_pack, gain_cross_grad, gain_final_grad,
     normed_two, hidden_two_low, slope, active, sum_ffn,
 ):
-    slices = w_inner.shape[0]
+    slices, units = pack_three.shape[0], pack_three.shape[1] // 2
+    w_out = Rows(pack_two, 4, cols)
     cross_low = cross_t[...].astype(BF16)
     normed, scale_two = layer_norm(hidden_one[...] + dot_tn(cross_low, w_out[...]))
     normed_two[...] = normed
@@ -195,11 +720,11 @@
     hidden_two_low[...] = hidden_two.astype(BF16)
     sum_ffn[...] = hidden_two
     for z in range(slices):
-        inner = dot_nn(hidden_two_low[...], w_inner[z])
+        inner = dot_nt(hidden_two_low[...], pack_three[z, 0:units, :])
         below = 0.5 * (1.0 + lax.erf(inner * math.sqrt(0.5)))
         slope[z] = below + inner * (jnp.exp2(inner * inner * (-0.5 * LOG2E)) * (1.0 / math.sqrt(2.0 * math.pi)))
         active[z] = (inner * below).astype(BF16)
-        sum_ffn[...] += dot_nn(active[z], w_outer[z])
+        sum_ffn[...] += dot_nn(active[z], pack_three[z, units:, :])
     normed_three, scale_three = layer_norm(sum_ffn[...])
     mixed[...] = (normed_three * gain_final[...]).astype(BF16)
     grad_three, gain_grad = norm_back(out_grad[...].astype(F32), normed_three, scale_three, gain_final[...])
@@ -207,10 +732,10 @@
     ffn_low = grad_three.astype(BF16)
     sum_ffn[...] = grad_three
     for z in range(slices):
-        w_outer_grad[z] = dot_tn(active[z], ffn_low).astype(BF16)
-        inner_low = (dot_nt(ffn_low, w_outer[z]) * slope[z]).astype(BF16)
-        w_inner_grad[z] = dot_tn(hidden_two_low[...], inner_low).astype(BF16)
-        sum_ffn[...] += dot_nt(inner_low, w_inner[z])
+        write_pieces(grad_three_pack, z, units, dot_tn(active[z], ffn_low))
+        inner_low = (dot_nt(ffn_low, pack_three[z, units:, :]) * slope[z]).astype(BF16)
+        write_pieces(grad_three_pack, z, 0, dot_tn(inner_low, hidden_two_low[...]))
+        sum_ffn[...] += dot_nn(inner_low, pack_three[z, 0:units, :])
     grad, gain_grad = norm_back(sum_ffn[...], normed_two[...], scale_two, gain_cross[...])
     gain_cross_grad[...] = gain_grad
     resid_grad[...] = grad
@@ -231,11 +756,11 @@
 
 
 def cross_back_kernel(
-    bounds, own, self_t, w_out, gain, resid_two_grad, w_cross_out, cross_t, lse, window, code, low, high,
-    w_query_t, w_key_t, w_value_t,
-    resid_one_grad, window_grad, w_query_grad, w_key_grad, w_value_grad, w_out_grad, gain_grad,
+    cols, bounds, own, self_t, gain, resid_two_grad, cross_t, lse, window, code, low, high, pack_two,
+    w_cross_out_grad, gain_cross_grad, gain_final_grad, resid_one_grad, window_grad, grad_two_pack,
     spread, grad_spread, pairs, grad_pairs, delta, bias, low_t, query_grad, key_sum, value_sum, normed_one, scale_one,
 ):
+    w_out, w_query_t, w_key_t, w_value_t, w_cross_out = (Rows(pack_two, k, cols) for k in range(5))
     self_low = self_t[...].astype(BF16)
     normed, scale = layer_norm(own[...].astype(F32) + dot_tn(self_low, w_out[...]))
     normed_one[...] = normed
@@ -251,23 +776,31 @@
         bounds, window, code, low, high, w_key_t, w_value_t, spread, grad_spread, pairs, grad_pairs, lse, delta, bias,
         query_grad, window_grad, key_sum, value_sum,
     )
-    w_key_grad[...] = key_sum[...].astype(BF16)
-    w_value_grad[...] = value_sum[...].astype(BF16)
     query_low = (query_grad[...] * SCALE).astype(BF16)
     hidden_low = (normed_one[...] * gain[...]).astype(BF16)
-    w_query_grad[...] = dot_nn(query_low, hidden_low).astype(BF16)
     grad_one = resid_two_grad[...] + dot_tn(query_low, w_query_t[...])
     grad, gain_sum = norm_back(grad_one, normed_one[...], scale_one[...], gain[...])
-    gain_grad[...] = gain_sum
     resid_one_grad[...] = grad
-    w_out_grad[...] = dot_nn(self_t[...].astype(BF16), grad.astype(BF16)).astype(BF16)
+    write_rows(grad_two_pack, 0, cols, dot_nn(self_t[...].astype(BF16), grad.astype(BF16)))
+    write_rows(grad_two_pack, 1, cols, dot_nn(query_low, hidden_low))
+    write_rows(grad_two_pack, 2, cols, key_sum[...].T)
+    write_rows(grad_two_pack, 3, cols, value_sum[...].T)
+    write_rows(grad_two_pack, 4, cols, w_cross_out_grad[...])
+    slices, rows, width = grad_two_pack.shape
+    gains = jnp.concatenate([gain_sum, gain_cross_grad[...], gain_final_grad[...], jnp.zeros((13, width), F32)], axis=0)
+    for z in range(slices):
+        grad_two_pack[z, 5 * cols : 5 * cols + 16, :] = gains.astype(BF16)
+        if rows > 5 * cols + 16:
+            grad_two_pack[z, 5 * cols + 16 :, :] = jnp.zeros((rows - 5 * cols - 16, width), BF16)
 
 
 def self_back_kernel(
-    bounds, own, resid_one_grad, w_out, self_t, lse, window, code, low, high, w_query_t, w_key_t, w_value_t,
-    own_grad, window_grad, w_query_grad, w_key_grad, w_value_grad,
+    cols, bounds, own, resid_one_grad, pack_two, self_t, lse, window, code, low, high, pack_one,
+    own_grad, window_grad, grad_one_pack,
     spread, grad_spread, pairs, grad_pairs, delta, bias, low_t, query_grad, key_sum, value_sum,
 ):
+    w_query_t, w_key_t, w_value_t = (Rows(pack_one, k, cols) for k in range(3))
+    w_out = Rows(pack_two, 0, cols)
     branch_low = resid_one_grad[...].astype(BF16)
     prepare_back(
         dot_nt(own[...], w_query_t[...]), dot_nt(w_query_t[...], own[...]),
@@ -278,14 +811,17 @@
         bounds, window, code, low, high, w_key_t, w_value_t, spread, grad_spread, pairs, grad_pairs, lse, delta, bias,
         query_grad, window_grad, key_sum, value_sum,
     )
-    w_key_grad[...] = key_sum[...].astype(BF16)
-    w_value_grad[...] = value_sum[...].astype(BF16)
     query_low = (query_grad[...] * SCALE).astype(BF16)
-    w_query_grad[...] = dot_nn(query_low, own[...]).astype(BF16)
+    write_rows(grad_one_pack, 0, cols, dot_nn(query_low, own[...]))
+    write_rows(grad_one_pack, 1, cols, key_sum[...].T)
+    write_rows(grad_one_pack, 2, cols, value_sum[...].T)
+    slices, rows, width = grad_one_pack.shape
+    if rows > 3 * cols:
+        grad_one_pack[:, 3 * cols :, :] = jnp.zeros((slices, rows - 3 * cols, width), BF16)
     own_grad[...] = (resid_one_grad[...] + dot_tn(query_low, w_query_t[...])).astype(BF16)
 
 
-def call(kernel, outs, scratch, smem, *args):
+def call(kernel, outs, scratch, smem, *args, micros=20):
     place = [pl.BlockSpec(memory_space=pltpu.SMEM)] * smem
     place += [pl.BlockSpec(memory_space=pltpu.VMEM)] * (len(args) - smem)
     return pl.pallas_call(
@@ -295,12 +831,24 @@
         out_specs=[pl.BlockSpec(memory_space=pltpu.VMEM)] * len(outs),
         scratch_shapes=[pltpu.VMEM(shape, kind) for shape, kind in scratch],
         compiler_params=pltpu.CompilerParams(vmem_limit_bytes=VMEM_LIMIT),
+        cost_estimate=pl.CostEstimate(flops=micros * 10**9, bytes_accessed=micros * 10**6, transcendentals=0),
     )(*args)
 
 
-def shifted(value, by):
-    peers = lax.axis_size("seq")
-    return lax.ppermute(value, "seq", [(i, i + by) for i in range(peers) if 0 <= i + by < peers])
+def padded(size, unit):
+    return -(-size // unit) * unit
+
+
+def talk(kernel, outs, out_space, scratch, copies, number, *args):
+    return pl.pallas_call(
+        kernel,
+        out_shape=[jax.ShapeDtypeStruct(shape, kind) for shape, kind in outs],
+        in_specs=[pl.BlockSpec(memory_space=pl.ANY)] * len(args),
+        out_specs=[pl.BlockSpec(memory_space=out_space)] * len(outs),
+        scratch_shapes=[pltpu.SemaphoreType.DMA((n,)) for n in (copies[0], copies[0], copies[1])] + [pltpu.VMEM(shape, kind) for shape, kind in scratch],
+        compiler_params=pltpu.CompilerParams(vmem_limit_bytes=VMEM_LIMIT, collective_id=number, has_side_effects=True),
+        cost_estimate=pl.CostEstimate(flops=80 * 10**9, bytes_accessed=80 * 10**6, transcendentals=0),
+    )(*args)
 
 
 def body(
@@ -335,109 +883,135 @@
     origin = begin - DOC_LEN
     bounds = jnp.stack([(first_row - origin) // CHUNK, (last_row - origin + CHUNK - 1) // CHUNK]).astype(jnp.int32)
 
-    def gathered(weight):
-        return lax.all_gather(weight, "head", axis=0, tiled=True)
-
-    def window_of(value):
-        below = shifted(value[rows - DOC_LEN :], 1)
-        above = shifted(value[:DOC_LEN], -1)
-        whole = jnp.concatenate([below, value, above, jnp.zeros((spare, width), value.dtype)], axis=0)
-        return lax.dynamic_slice_in_dim(whole, part * count, wide, 0)
-
     own = lax.dynamic_slice_in_dim(query_state, part * count, count, 0)
     own_out_grad = lax.dynamic_slice_in_dim(out_grad, part * count, count, 0)
-    w_query_t, w_key_t, w_value_t = gathered(w_query.T), gathered(w_key.T), gathered(w_value.T)
-    content_window = window_of(content)
-    w_out_all = gathered(w_out)
-    w_cross_query_t = gathered(w_cross_query.T)
-    w_cross_key_t, w_cross_value_t = gathered(w_cross_key.T), gathered(w_cross_value.T)
-    encoded_window = window_of(encoded)
-    w_cross_out_all = gathered(w_cross_out)
-    w_inner_all = lax.all_gather(w_inner, "head", axis=0)
-    w_outer_all = lax.all_gather(w_outer, "head", axis=0)
     gain_self, gain_cross, gain_final = (g.reshape(1, width) for g in (gain_self, gain_cross, gain_final))
+
+    peers = lax.axis_size("seq")
+    chips = peers // 2
+    cols, units = w_query.shape[1], w_inner.shape[1]
+    unit = 16 * peers
+    sizes = [padded(n, unit) for n in (3 * cols, 5 * cols, 2 * units)]
+    grad_sizes = [sizes[0], padded(5 * cols + 16, unit), sizes[2]]
+
+    def packed(size, *weights):
+        used = sum(w.shape[0] for w in weights)
+        return jnp.concatenate(list(weights) + [jnp.zeros((size - used, width), BF16)] * (size > used), axis=0)
+
+    packs = (
+        packed(sizes[0], w_query.T, w_key.T, w_value.T),
+        packed(sizes[1], w_out, w_cross_query.T, w_cross_key.T, w_cross_value.T, w_cross_out),
+        packed(sizes[2], w_inner.T, w_outer),
+    )
+    start_copies = 3 * (slices - 1) * (2 * chips) + 4 * slices
+    content_window, encoded_window, pack_one, pack_two, pack_three = talk(
+        partial(start_kernel, peers, slices, count),
+        [((wide, width), BF16)] * 2 + [((slices, n, width), BF16) for n in sizes], pltpu.VMEM,
+        [((DOC_LEN, width), BF16)], (start_copies, 8 * slices + 8), 0, content, encoded, *packs,
+    )
+
+    def split_refs(kernel, ins, outs):
+        def run(*refs):
+            return kernel(refs[:ins], refs[ins : ins + outs], refs[ins + outs :])
+        return run
 
     stats = [((HEADS * PAIR, count), BF16), ((CHUNK, count), F32), ((HEADS, count), F32), ((HEADS, count), F32), ((width, count), BF16)]
     self_t, lse_self = call(
-        self_kernel, [((width, count), F32), ((HEADS, count), F32)], stats, 1,
-        bounds, own, content_window, code, low, high_self, w_query_t, w_key_t, w_value_t,
+        partial(self_kernel, cols), [((width, count), F32), ((HEADS, count), F32)], stats, 1,
+        bounds, own, content_window, code, low, high_self, pack_one,
     )
     hidden_one, cross_t, lse_cross = call(
-        cross_kernel, [((count, width), F32), ((width, count), F32), ((HEADS, count), F32)], stats, 1,
-        bounds, own, self_t, w_out_all, gain_self, encoded_window, code, low, high_cross,
-        w_cross_query_t, w_cross_key_t, w_cross_value_t,
-    )
-    hidden_units = w_inner.shape[1]
-    mixed, resid_two_grad, w_cross_out_grad, w_inner_grad, w_outer_grad, gain_cross_grad, gain_final_grad = call(
-        ffn_kernel,
+        partial(cross_kernel, cols), [((count, width), F32), ((width, count), F32), ((HEADS, count), F32)], stats, 1,
+        bounds, own, self_t, gain_self, encoded_window, code, low, high_cross, pack_two,
+    )
+    mixed, resid_two_grad, w_cross_out_grad, grads_three, gain_cross_grad, gain_final_grad = call(
+        partial(ffn_kernel, cols),
         [
-            ((count, width), BF16), ((count, width), F32), ((width, width), BF16), ((slices, width, hidden_units), BF16),
-            ((slices, hidden_units, width), BF16), ((1, width), F32), ((1, width), F32),
+            ((count, width), BF16), ((count, width), F32), ((width, width), BF16), ((peers, slices, grad_sizes[2] // peers, width), BF16),
+            ((1, width), F32), ((1, width), F32),
         ],
         [
-            ((count, width), F32), ((count, width), BF16), ((slices, count, hidden_units), F32),
-            ((slices, count, hidden_units), BF16), ((count, width), F32),
+            ((count, width), F32), ((count, width), BF16), ((slices, count, units), F32),
+            ((slices, count, units), BF16), ((count, width), F32),
         ], 0,
-        hidden_one, cross_t, w_cross_out_all, gain_cross, w_inner_all, w_outer_all, gain_final, own_out_grad,
+        hidden_one, cross_t, pack_two, gain_cross, pack_three, gain_final, own_out_grad,
     )
     back = [
         ((HEADS * PAIR, count), BF16), ((HEADS * PAIR, count), BF16), ((PAIRS, 2 * count, PAIR), BF16),
         ((PAIRS, 2 * count, PAIR), BF16), ((HEADS, count), F32), ((CHUNK, count), F32), ((width, count), BF16),
         ((width, count), F32), ((width, width), F32), ((width, width), F32),
     ]
-    square = ((width, width), BF16)
-    resid_one_grad, encoded_part, w_cross_query_grad, w_cross_key_grad, w_cross_value_grad, w_out_grad, gain_self_grad = call(
-        cross_back_kernel,
-        [((count, width), F32), ((wide, width), BF16), square, square, square, square, ((1, width), F32)],
+    resid_one_grad, encoded_part, grads_two = call(
+        partial(cross_back_kernel, cols),
+        [((count, width), F32), ((wide, width), BF16), ((slices, grad_sizes[1], width), BF16)],
         back + [((count, width), F32), ((count, 1), F32)], 1,
-        bounds, own, self_t, w_out_all, gain_self, resid_two_grad, w_cross_out_all, cross_t, lse_cross,
-        encoded_window, code, low, high_cross, w_cross_query_t, w_cross_key_t, w_cross_value_t,
-    )
-    own_grad, content_part, w_query_grad, w_key_grad, w_value_grad = call(
-        self_back_kernel, [((count, width), BF16), ((wide, width), BF16), square, square, square], back, 1,
-        bounds, own, resid_one_grad, w_out_all, self_t, lse_self,
-        content_window, code, low, high_self, w_query_t, w_key_t, w_value_t,
-    )
-
-    def returned(grad):
-        place = jnp.zeros((2 * DOC_LEN + rows + spare, width), BF16)
-        place = lax.dynamic_update_slice_in_dim(place, grad, part * count, 0)
-        below = shifted(place[:DOC_LEN], -1).astype(F32)
-        above = shifted(place[DOC_LEN + rows : 2 * DOC_LEN + rows], 1).astype(F32)
-        whole = place[DOC_LEN : DOC_LEN + rows].astype(F32)
-        whole = whole + jnp.pad(below, ((rows - DOC_LEN, 0), (0, 0))) + jnp.pad(above, ((0, rows - DOC_LEN), (0, 0)))
-        return lax.psum(whole.astype(BF16), "head").astype(F32)
-
-    def summed(grad):
-        return lax.psum(lax.psum_scatter(grad, "head", scatter_dimension=0, tiled=True), "seq").astype(F32)
-
-    def summed_t(grad):
-        return summed(grad).T
-
-    def summed_columns(grad):
-        return lax.psum(lax.psum_scatter(grad, "head", scatter_dimension=1, tiled=True), "seq").astype(F32)
-
-    def summed_gain(grad):
-        return lax.psum(grad.reshape(width), ("seq", "head"))
-
+        bounds, own, self_t, gain_self, resid_two_grad, cross_t, lse_cross, encoded_window, code, low, high_cross, pack_two,
+        w_cross_out_grad, gain_cross_grad, gain_final_grad, micros=35,
+    )
+    own_grad, content_part, grads_one = call(
+        partial(self_back_kernel, cols),
+        [((count, width), BF16), ((wide, width), BF16), ((slices, grad_sizes[0], width), BF16)], back, 1,
+        bounds, own, resid_one_grad, pack_two, self_t, lse_self, content_window, code, low, high_self, pack_one, micros=35,
+    )
+
+    mixed = lax.all_gather(mixed, "head", axis=0, tiled=True)
+    plane_three = lax.psum_scatter(grads_three, "seq", scatter_dimension=0, tiled=True).reshape(grads_three.shape[1:])
+    blocks, parts, grads, planes = [own_grad], [content_part, encoded_part], [grads_one, grads_two], [plane_three]
+    weight_scratch = []
+    for n in grad_sizes[: len(grads)]:
+        half, size = n // 2, n // 2 // chips
+        weight_scratch += [
+            ((slices, half, width), BF16), ((slices, half, width), BF16), ((chips - 1, slices, size, width), BF16),
+            ((slices, size, width), BF16), ((slices - 1, size, width), BF16),
+        ]
+    halves = 2 if slices <= 4 else 1
+    units_in = (slices - 1) * halves
+    part_scratch = [
+        ((rows, width), BF16), ((DOC_LEN, width), BF16), ((DOC_LEN, width), BF16),
+        ((units_in, count // halves, width), BF16), ((units_in, count // halves, width), BF16),
+    ] * len(parts)
+    plane_scratch = []
+    for n in grad_sizes[len(grads) :]:
+        plane_scratch += [((slices, n // peers, width), BF16), ((slices - 1, n // peers, width), BF16)]
+    ins, outs = (len(blocks), len(parts), len(grads), len(planes)), (len(blocks), len(parts), len(grad_sizes))
+
+    def end(refs, out_refs, scratch):
+        a, b, c = ins[0], ins[0] + ins[1], sum(ins[:3])
+        end_kernel(
+            peers, slices, count, refs[:a], refs[a:b], refs[b:c], refs[c:], out_refs[: outs[0]],
+            out_refs[outs[0] : outs[0] + outs[1]], out_refs[outs[0] + outs[1] :], scratch,
+        )
+
+    end_copies = len(grad_sizes) * (1 + 3 * (chips - 1) + slices) + len(parts) * 2 * slices + (len(blocks) + 2 * len(parts)) * 2 * slices * halves
+    results = talk(
+        split_refs(end, sum(ins), sum(outs)),
+        [((rows, width), BF16)] * (len(blocks) + len(parts)) + [((n, width), BF16) for n in grad_sizes], pltpu.VMEM,
+        weight_scratch + part_scratch + plane_scratch, (end_copies, 8 * slices + 8), 1, *blocks, *parts, *grads, *planes,
+    )
+    query_state_grad, content_grad, encoded_grad, sum_one, sum_two, sum_three = results
+
+    def rows_of(pack, k):
+        return pack[k * cols : (k + 1) * cols].astype(F32)
+
+    gains = sum_two[5 * cols : 5 * cols + 16].astype(F32)
     return (
-        lax.all_gather(mixed, "head", axis=0, tiled=True),
-        lax.all_gather(own_grad, "head", axis=0, tiled=True).astype(F32),
-        returned(content_part),
-        returned(encoded_part),
-        summed_t(w_query_grad),
-        summed_columns(w_key_grad),
-        summed_columns(w_value_grad),
-        summed(w_out_grad),
-        summed_gain(gain_self_grad),
-        summed_t(w_cross_query_grad),
-        summed_columns(w_cross_key_grad),
-        summed_columns(w_cross_value_grad),
-        summed(w_cross_out_grad),
-        summed_gain(gain_cross_grad),
-        lax.psum(lax.psum_scatter(w_inner_grad, "head", scatter_dimension=0, tiled=False), "seq").astype(F32),
-        lax.psum(lax.psum_scatter(w_outer_grad, "head", scatter_dimension=0, tiled=False), "seq").astype(F32),
-        summed_gain(gain_final_grad),
+        mixed,
+        query_state_grad.astype(F32),
+        content_grad.astype(F32),
+        encoded_grad.astype(F32),
+        rows_of(sum_one, 0).T,
+        rows_of(sum_one, 1).T,
+        rows_of(sum_one, 2).T,
+        rows_of(sum_two, 0),
+        gains[0],
+        rows_of(sum_two, 1).T,
+        rows_of(sum_two, 2).T,
+        rows_of(sum_two, 3).T,
+        rows_of(sum_two, 4),
+        gains[1],
+        sum_three[:units].astype(F32).T,
+        sum_three[units : 2 * units].astype(F32),
+        gains[2],
     )
 
 

time: 918 us -> 459 us (0.50)
  the two profiles are of different devices: /device:TPU:0 before, /device:TPU:27 now
where the time goes in v2:
time: 459 us; the launch traced here: 460 us
  Pallas kernels  401 us (87%)
  local copies, waits for them, and re-layouts  23.2 us (5%)
  other arithmetic  17.4 us (4%)
  between operations  17.1 us (4%)
    pallas_call x2, Pallas kernels, talk(): pl.pallas_call(kernel, out_shape=[jax.ShapeDtypeStruct(shape, kind) for s...  268 us
    pallas_call x5, Pallas kernels, call(): pl.pallas_call(kernel, out_shape=[jax.ShapeDtypeStruct(shape, kind) for s...  133 us
    unnamed x41, local copies, waits for them, and re-layouts  14.9 us
  transfers between devices with their start and end apart: 2, of which 0 were waited for; matrix products, arithmetic and copies ran while one was open for 0% of the time, Pallas kernels for 16%

profile of v2, /device:TPU:27, one launch (start us, length us, event | category | flops | bytes accessed | tf_op | source)
XLA Modules:
  0.0 459.6 jit_solution(15060655324223493282)
XLA Ops:
  9.5 1.2 fusion
  11.3 2.0 fusion.11
  17.6 1.0 copy.69
  18.6 1.0 copy.70
  19.6 1.0 copy.71
  20.6 1.0 copy.72
  21.6 1.0 copy.73
  22.6 1.0 copy.74
  23.6 1.3 copy.75
  25.0 2.0 reshape.88.code
  27.6 1.0 pad_maximum_fusion.pack_three
  28.7 0.8 pad_maximum_fusion.1.pack_one
  29.6 2.0 constant_dynamic-slice_fusion
  31.6 67.9 %shard_map.323 = (bf16[2560,512]{1,0:T(8,128)(2,1)}, bf16[2560,512]{1,0:T(8,128)(2,1)}, bf16[4,384,512]{2,1,0:T(8,128)(2,1)}, bf16[4,640,512]{2,1,0:T(8,128)(2,1)}, bf16[4,1024,512]{2,1,0:T(8,128)(2,1)}) custom-call(bf16[1536,512]{1,0:T(8,128)(2,1)} %content.1, bf16[1536,512]{1,0:T(8,128)(2,1)} %encoded.1, bf16[384,512]{1,0:T(8,128)(2,1)} %pad_maximum_fusion.1.pack_one, ...), custom_call_target="tpu_custom_call" | custom-call | flops 80000000000 | bytes 80000000 | tf_op jit(solution)/shard_map/pallas_call | solution.py:843
  99.5 22.5 %shard_map.324 = (f32[512,384]{1,0:T(8,128)}, f32[8,384]{1,0:T(8,128)}) custom-call(s32[2]{0:T(128)} %pad_add_fusion.bounds, bf16[384,512]{1,0:T(8,128)(2,1)} %get-tuple-element.142.own, bf16[2560,512]{1,0:T(8,128)(2,1)} %get-tuple-element.45.window, s32[2560,1]{1,0:T(8,128)} %reshape.88.code, s32[1,384]{1,0:T(1,128)} %reshape.81.low, ...), custom_call_target="tpu_custom_call" | custom-call | flops 20000000000 | bytes 20000000 | tf_op jit(solution)/shard_map/pallas_call | solution.py:827
  122.1 24.1 %shard_map.325 = (f32[384,512]{1,0:T(8,128)}, f32[512,384]{1,0:T(8,128)}, f32[8,384]{1,0:T(8,128)}) custom-call(s32[2]{0:T(128)} %pad_add_fusion.bounds, bf16[384,512]{1,0:T(8,128)(2,1)} %get-tuple-element.142.own, f32[512,384]{1,0:T(8,128)} %get-tuple-element.47.attn_t.self_t, f32[1,512]{1,0:T(1,128)} %bitcast.51, ...), custom_call_target="tpu_custom_call" | custom-call | flops 20000000000 | bytes 20000000 | tf_op jit(solution)/shard_map/pallas_call | solution.py:827
  146.1 13.5 %shard_map.326 = (bf16[384,512]{1,0:T(8,128)(2,1)}, f32[384,512]{1,0:T(8,128)}, bf16[512,512]{1,0:T(8,128)(2,1)}, bf16[8,4,128,512]{3,2,1,0:T(8,128)(2,1)}, f32[1,512]{1,0:T(1,128)}, /*index=5*/f32[1,512]{1,0:T(1,128)}) custom-call(f32[384,512]{1,0:T(8,128)} %get-tuple-element.50.hidden_one, f32[512,384]{1,0:T(8,128)} %get-tuple-element.51.cross_t, ...), custom_call_target="tpu_custom_call" | custom-call | flops 20000000000 | bytes 20000000 | tf_op jit(solution)/shard_map/pallas_call | solution.py:827
  160.2 37.5 %shard_map.327 = (f32[384,512]{1,0:T(8,128)}, bf16[2560,512]{1,0:T(8,128)(2,1)}, bf16[4,768,512]{2,1,0:T(8,128)(2,1)}) custom-call(s32[2]{0:T(128)} %pad_add_fusion.bounds, bf16[384,512]{1,0:T(8,128)(2,1)} %get-tuple-element.142.own, f32[512,384]{1,0:T(8,128)} %get-tuple-element.47.attn_t.self_t, f32[1,512]{1,0:T(1,128)} %bitcast.52, ...), custom_call_target="tpu_custom_call" | custom-call | flops 35000000512 | bytes 35000000 | tf_op jit(solution)/shard_map/pallas_call | solution.py:827
  197.7 35.9 %shard_map.328 = (bf16[384,512]{1,0:T(8,128)(2,1)}, bf16[2560,512]{1,0:T(8,128)(2,1)}, bf16[4,384,512]{2,1,0:T(8,128)(2,1)}) custom-call(s32[2]{0:T(128)} %pad_add_fusion.bounds, bf16[384,512]{1,0:T(8,128)(2,1)} %get-tuple-element.142.own, f32[384,512]{1,0:T(8,128)} %get-tuple-element.59.resid_one_grad, bf16[4,640,512]{2,1,0:T(8,128)(2,1)} %get-tuple-element.49.pack_two, ...), custom_call_target="tpu_custom_call" | custom-call | flops 35000000512 | bytes 35000000 | tf_op jit(solution)/shard_map/pallas_call | solution.py:827
  233.6 199.9 %shard_map.329 = (bf16[1536,512]{1,0:T(8,128)(2,1)}, bf16[1536,512]{1,0:T(8,128)(2,1)}, bf16[1536,512]{1,0:T(8,128)(2,1)}, bf16[384,512]{1,0:T(8,128)(2,1)}, bf1...) custom-call(bf16[384,512]{1,0:T(8,128)(2,1)} %get-tuple-element.61.refs_0_, ...), custom_call_target="tpu_custom_call" | custom-call | flops 80000000000 | bytes 80000000 | tf_op jit(solution)/shard_map/pallas_call | solution.py:843
  434.3 2.1 slice_convert_fusion.1
  437.0 0.8 copy.85
  437.9 0.8 copy.84
  438.7 0.8 copy.83
  439.6 0.8 copy.82
  441.3 0.8 copy.80
  442.1 2.1 convert_element_type.32
  444.3 1.3 slice_convert_fusion
  445.5 1.3 copy.86
  446.8 2.1 convert_element_type.33
  448.9 2.1 convert_element_type.34
  451.0 1.1 copy.92
  (52 shorter events, 8.6 us)
Async XLA Ops:
  8.0 16.9 %copy-start.7 = (bf16[128,512]{1,0:T(8,128)(2,1)S(1)}, bf16[128,512]{1,0:T(8,128)(2,1)}, u32[]{:S(2)}) copy-start(bf16[128,512]{1,0:T(8,128)(2,1)} %param.29) | copy-start | bytes 393220
  8.0 16.9 %copy-start.9 = (s32[12288]{0:T(1024)S(1)}, s32[12288]{0:T(1024)}, u32[]{:S(2)}) copy-start(s32[12288]{0:T(1024)} %param.24) | copy-start | bytes 147460
  8.0 19.6 %copy-start.5 = (bf16[512,512]{1,0:T(8,128)(2,1)S(1)}, bf16[512,512]{1,0:T(8,128)(2,1)}, u32[]{:S(2)}) copy-start(bf16[512,512]{1,0:T(8,128)(2,1)} %param.37) | copy-start | bytes 1572868
  8.1 225.6 %all-gather.2.cloned.1.call-start = ((), (), s32[]{:S(2)}) async-start(), calls=%async_computation.1 | async-start | bytes 1966080 | tf_op jit(solution)/shard_map/all_gather | solution.py:957
  24.9 3.8 copy-start.8
  28.7 2.9 copy-start.10
  159.6 74.0 %reduce-scatter.2.cloned.1.call-start = ((), (), s32[]{:S(2)}) async-start(), calls=%async_computation.2 | async-start | bytes 4718592 | tf_op jit(solution)/shard_map/reduce_scatter | solution.py:958
  433.5 6.0 %copy-start.6 = (bf16[384,512]{1,0:T(8,128)(2,1)S(1)}, bf16[384,512]{1,0:T(8,128)(2,1)}, u32[]{:S(2)}) copy-start(bf16[384,512]{1,0:T(8,128)(2,1)} %get-tuple-element.70) | copy-start | bytes 1179652
  436.4 5.7 %copy-start.3 = (bf16[1536,512]{1,0:T(8,128)(2,1)S(1)}, bf16[1536,512]{1,0:T(8,128)(2,1)}, u32[]{:S(2)}) copy-start(bf16[1536,512]{1,0:T(8,128)(2,1)} %get-tuple-element.67) | copy-start | bytes 4718596
  442.1 2.1 copy-start.4
  444.3 2.6 copy-start.2
  446.8 2.1 copy-start.1
  448.9 2.1 copy-start
Sparse Core Ops, SparseCore 0:
  159.8 44.7 all-gather.1
Sparse Core Ops, SparseCore 1:
  163.5 60.6 reduce-scatter.1
